TPU v7x, 128 devices: a whole 4x4x4 slice. The times are simulated.
128 devices in a mesh: frag: 8 (over x, core), grid: 16 (over y, z).
Axes of the slice: x: 4, y: 4, z: 4, core: 2. Of those that a mesh axis runs over, the one named last changes fastest.
Arguments:
- kinetic: bfloat16 [256, 1024, 1024], P(('frag', 'grid')), may hold values from -1 to 4, as said below
- basis: bfloat16 [256, 2048, 1024], P(('frag', 'grid')), may hold values from -0.1875 to 0.1875
- start_orbitals: bfloat16 [256, 1024, 128], P(('frag', 'grid')), may hold values from -6 to 6
- background: float32 [256, 256, 256], P('frag', 'grid'), may hold values from -2 to 2
- tile_ids: int32 [256, 8], P(('frag', 'grid')), may hold values from 0 to 65535, as said below
- tile_counts: int32 [256], P(('frag', 'grid')), may hold values from 6 to 8, as said below
- degrees: int32 [256], P(('frag', 'grid')), may hold values from 1 to 2
Outputs:
- potential: float32 [256, 256, 256], P('frag', 'grid')
- density_out: float32 [256, 256, 256], P('frag', 'grid')
Inputs may be any that keep to these rules, and one draw needn't show every extreme that they name: `kinetic`: each fragment's matrix is symmetric. `tile_ids`: fragments lie 2 to a device in the order of frag+grid. A fragment's live lines are distinct, and their x lies in the block of 32 planes of the fragment's index of frag. Among the live lines of one device's fragments at most 2 have y in any one block of 16 rows, and on every device exactly 2 do for some block. `tile_counts`: every device holds a fragment with 8 live tiles.
All inputs are finite; a program needn't handle non-finite values.
Results may differ from a plain program's by a relative error of at most 0.002.
Values sent between devices are 32-bit elements; how exact they have to be, the bound alone decides.
No kernel may reach another device: no remote copies, remote signals or barrier semaphores. Data moves between devices by JAX's collectives and lax.ppermute only.
A program may use at most 128 MiB of HBM per device.

v0:
```python
import jax
import jax.numpy as jnp
from jax import lax
from jax.sharding import PartitionSpec as P

CAP = 2
STEPS = 2


filter_center = 5.0
filter_half = 4.0
full_precision = lax.Precision.HIGHEST


def sine_rows(row_index, length):
    column = jnp.arange(length, dtype=jnp.int32) + 1
    phase = (row_index + 1)[:, None] * column[None, :] % (2 * (length + 1))
    angle = jnp.pi * phase.astype(jnp.float32) / (length + 1)
    return jnp.sqrt(jnp.float32(2.0 / (length + 1))) * jnp.sin(angle)


def eigen_line(row_index, length):
    return 2.0 - 2.0 * jnp.cos(jnp.pi * (row_index + 1).astype(jnp.float32) / (length + 1))


def orthonormalize(block):
    gram = jnp.dot(block.T, block, precision=full_precision)
    factor = jnp.linalg.cholesky(gram)
    return jax.scipy.linalg.solve_triangular(factor, block.T, lower=True).T


def apply_hamiltonian(kinetic_f, basis_f, field_f, vector):
    collocated = jnp.dot(basis_f, vector, preferred_element_type=jnp.float32)
    weighted = (field_f[:, None] * collocated).astype(jnp.bfloat16)
    local_part = jnp.dot(kinetic_f, vector, preferred_element_type=jnp.float32)
    grid_part = lax.dot_general(
        basis_f, weighted, (((0,), (0,)), ((), ())), preferred_element_type=jnp.float32
    )
    return local_part + grid_part


def next_term(kinetic_f, basis_f, field_f, current, earlier):
    rounded = current.astype(jnp.bfloat16)
    following = 2.0 * (
        apply_hamiltonian(kinetic_f, basis_f, field_f, rounded)
        - filter_center * rounded.astype(jnp.float32)
    ) / filter_half - earlier.astype(jnp.float32)
    return (following, rounded)


def filter_step(item):
    kinetic_f, basis_f, field_f, degree, orbitals = item
    earlier = orbitals.astype(jnp.bfloat16)
    current = (
        apply_hamiltonian(kinetic_f, basis_f, field_f, earlier)
        - filter_center * earlier.astype(jnp.float32)
    ) / filter_half
    chosen = current
    following, rounded = next_term(kinetic_f, basis_f, field_f, current, earlier)
    chosen = jnp.where(degree == 2, following, chosen)
    return orthonormalize(chosen)


def density_rows(basis_f, orbitals):
    values = jnp.dot(basis_f, orbitals.astype(jnp.bfloat16), preferred_element_type=jnp.float32)
    return 2.0 * jnp.sum(values * values, axis=1)


def spectral(source):
    groups = lax.axis_size("frag")
    owners = lax.axis_size("grid")
    group_index = lax.axis_index("frag")
    owner_index = lax.axis_index("grid")
    planes_dev, rows_dev, depth = source.shape
    width_x = planes_dev * groups
    width_y = rows_dev * owners
    table_x = sine_rows(jnp.arange(width_x, dtype=jnp.int32), width_x)
    table_y = sine_rows(jnp.arange(width_y, dtype=jnp.int32), width_y)
    table_z = sine_rows(jnp.arange(depth, dtype=jnp.int32), depth)
    flat_source = source.reshape(-1, depth)
    spectrum = jnp.dot(flat_source, table_z, precision=full_precision).reshape(
        planes_dev, rows_dev, depth
    )
    rows_out = lax.all_to_all(spectrum, "grid", split_axis=2, concat_axis=1, tiled=True)
    rows_out = jnp.einsum("bj,ajk->abk", table_y, rows_out, precision=full_precision)
    columns = lax.all_to_all(rows_out, "frag", split_axis=1, concat_axis=0, tiled=True)
    columns = jnp.einsum("ai,ijk->ajk", table_x, columns, precision=full_precision)
    row_index = group_index * (width_y // groups) + jnp.arange(width_y // groups, dtype=jnp.int32)
    depth_index = owner_index * (depth // owners) + jnp.arange(depth // owners, dtype=jnp.int32)
    eigen = (
        eigen_line(jnp.arange(width_x, dtype=jnp.int32), width_x)[:, None, None]
        + eigen_line(row_index, width_y)[None, :, None]
    )
    eigen = eigen + eigen_line(depth_index, depth)[None, None, :]
    columns = columns / eigen
    columns = jnp.einsum("ai,ijk->ajk", table_x, columns, precision=full_precision)
    rows_back = lax.all_to_all(columns, "frag", split_axis=0, concat_axis=1, tiled=True)
    rows_back = jnp.einsum("bj,ajk->abk", table_y, rows_back, precision=full_precision)
    returned = lax.all_to_all(rows_back, "grid", split_axis=1, concat_axis=2, tiled=True)
    result = jnp.dot(returned.reshape(-1, depth), table_z, precision=full_precision)
    return result.reshape(planes_dev, rows_dev, depth)


def shards(kinetic, basis, start_orbitals, background, tile_ids, tile_counts, degrees):
    owners = lax.axis_size("grid")
    group_index = lax.axis_index("frag")
    planes_dev, rows_dev, depth = background.shape
    width_y = rows_dev * owners
    frag_dev, tile_max = tile_ids.shape
    entries = frag_dev * tile_max
    slots = owners * CAP
    live = jnp.arange(tile_max, dtype=jnp.int32)[None, :] < tile_counts[:, None]
    live_rows = jnp.repeat(live.astype(jnp.float32), depth, axis=1)
    live_flat = live.reshape(-1)
    lines = tile_ids.reshape(-1)
    column_y = lines % width_y
    target = column_y // rows_dev
    local_line = (lines // width_y - group_index * planes_dev) * rows_dev + column_y % rows_dev
    position = jnp.arange(entries, dtype=jnp.int32)
    earlier = (
        (target[:, None] == target[None, :])
        & (position[None, :] < position[:, None])
        & live_flat[None, :]
    )
    rank = jnp.sum(earlier.astype(jnp.int32), axis=1)
    slot_of = target * CAP + rank
    picks = (jnp.arange(slots, dtype=jnp.int32)[:, None] == slot_of[None, :]) & live_flat[None, :]
    pick_matrix = picks.astype(jnp.float32)
    sent_lines = jnp.sum(jnp.where(picks, local_line[None, :] + 1, 0), axis=1) - 1
    cell_index = jnp.arange(planes_dev * rows_dev, dtype=jnp.int32)

    def tile_trade(values):
        return (
            lax.all_to_all(values, "grid", split_axis=0, concat_axis=0, tiled=True),
            lax.all_to_all(sent_lines, "grid", split_axis=0, concat_axis=0, tiled=True),
        )

    def to_owners(rows):
        packed = jnp.dot(pick_matrix, rows, precision=full_precision)
        arrived, arrived_lines = tile_trade(packed)
        placing = (cell_index[:, None] == arrived_lines[None, :]).astype(jnp.float32)
        summed = jnp.dot(placing, arrived, precision=full_precision)
        return (summed.reshape(planes_dev, rows_dev, depth), placing)

    def initial(item):
        basis_f, start_f, live_f, count_f = item
        orbitals = orthonormalize(start_f.astype(jnp.float32))
        density = density_rows(basis_f, orbitals) * live_f
        mean_value = jnp.sum(density) / (count_f * depth).astype(jnp.float32)
        return (orbitals, (density - mean_value) * live_f)

    orbitals, charge = lax.map(initial, (basis, start_orbitals, live_rows, tile_counts))
    grid_charge, placing = to_owners(charge.reshape(entries, depth))
    potential = spectral(grid_charge - background)
    lines_back = jnp.dot(placing.T, potential.reshape(-1, depth), precision=full_precision)
    returned, ignored = tile_trade(lines_back)
    field = jnp.dot(pick_matrix.T, returned, precision=full_precision).reshape(
        frag_dev, tile_max * depth
    )
    for step in range(STEPS):
        orbitals = lax.map(filter_step, (kinetic, basis, field, degrees, orbitals))
    final = lax.map(
        lambda item: density_rows(item[0], item[1]) * item[2], (basis, orbitals, live_rows)
    )
    density_out, unused_placing = to_owners(final.reshape(entries, depth))
    return (potential, density_out)


def solution(mesh):
    in_specs = (
        P(("frag", "grid"), None, None),
        P(("frag", "grid"), None, None),
        P(("frag", "grid"), None, None),
        P("frag", "grid", None),
        P(("frag", "grid"), None),
        P(("frag", "grid")),
        P(("frag", "grid")),
    )
    out_specs = (P("frag", "grid", None), P("frag", "grid", None))
    return jax.shard_map(shards, mesh=mesh, in_specs=in_specs, out_specs=out_specs, check_vma=False)
```

profile of v0, /device:TPU:0, one launch (start us, length us, event | category | flops | bytes accessed | tf_op | source)
XLA Modules:
  0.0 419.4 jit_solution(4556879176302755926)
XLA Ops:
  3.2 8.1 %all-to-all-start = ((s32[16,2,1]{1,2,0:T(1,128)}), s32[16,2,1]{1,2,0:T(1,128)S(1)}, u32[]{:S(2)}, u32[]{:S(2)}) async-start(s32[16,2,1]{1,2,0:T(1,128)} %bitcast.37), calls=%async_computation | async-start | bytes 16384 | tf_op jit(solution)/shard_map/all_to_all | solution.py:135
  11.6 64.9 %while.46 = (s32[]{:T(128)}, bf16[2,1024,128]{1,2,0:T(8,128)(2,1)S(1)}, f32[2,2048]{1,0:T(2,128)S(1)}, bf16[2,1024,128]{2,1,0:T(8,128)(2,1)}, bf16[2,2048,1024]{...) while((s32[]{:T(128)}, ...), condition=%wide.region_7.10_spmd, body=%wide.region_2.9_spmd.sunk | while | flops 772565120 | bytes 6253795 | solution.py:152
  13.0 11.7 %cholesky.182 = f32[128,128]{1,0:T(8,128)S(1)} custom-call(f32[128,128]{1,0:T(8,128)S(1)} %fusion.341), custom_call_target="Cholesky" | custom-call | tf_op jit(solution)/shard_map/while/body/eval_jaxpr/jit(cholesky)/cholesky | solution.py:28
  26.2 9.8 %custom-call.13 = f32[1,128,128]{1,2,0:T(8,128)S(1)} custom-call(f32[1,128,128]{2,1,0:T(8,128)S(1)} %fusion.342), custom_call_target="InvertDiagBlocksLowerTriangular" | custom-call | tf_op jit(solution)/shard_map/while/body/eval_jaxpr/jit(_solve_triangular)/triangular_solve | solution.py:29
  45.4 11.7 %cholesky.182 = f32[128,128]{1,0:T(8,128)S(1)} custom-call(f32[128,128]{1,0:T(8,128)S(1)} %fusion.341), custom_call_target="Cholesky" | custom-call | tf_op jit(solution)/shard_map/while/body/eval_jaxpr/jit(cholesky)/cholesky | solution.py:28
  58.6 9.8 %custom-call.13 = f32[1,128,128]{1,2,0:T(8,128)S(1)} custom-call(f32[1,128,128]{2,1,0:T(8,128)S(1)} %fusion.342), custom_call_target="InvertDiagBlocksLowerTriangular" | custom-call | tf_op jit(solution)/shard_map/while/body/eval_jaxpr/jit(_solve_triangular)/triangular_solve | solution.py:29
  96.9 13.2 %all_to_all.106 = f32[16,1,8192]{2,1,0:T(1,128)S(1)} all-to-all(f32[16,1,8192]{2,1,0:T(1,128)S(1)} %reshape.421), channel_id=1, replica_groups=mesh['frag'=8,'grid'=16] {'grid'}, dimensions={0} | all-to-all | bytes 1048576 | tf_op jit(solution)/shard_map/all_to_all | solution.py:84
  127.6 10.1 %all-to-all-done.3 = f32[8,1,16384]{2,1,0:T(1,128)S(1)} async-done(((f32[8,1,16384]{2,1,0:T(1,128)}), f32[8,1,16384]{2,1,0:T(1,128)S(1)}, u32[]{:S(2)}, u32[]{:S(2)}) %all-to-all-start.3) | async-done | bytes 524320 | tf_op jit(solution)/shard_map/all_to_all | solution.py:86
  150.8 13.0 %all_to_all.107 = f32[8,1,16384]{2,1,0:T(1,128)S(1)} all-to-all(f32[8,1,16384]{2,1,0:T(1,128)S(1)} %reshape.425), channel_id=1, replica_groups=mesh['frag'=8,'grid'=16] {'frag'}, dimensions={0} | all-to-all | bytes 1048576 | tf_op jit(solution)/shard_map/all_to_all | solution.py:97
  175.1 14.4 %all_to_all.108 = f32[16,1,8192]{2,1,0:T(1,128)S(1)} all-to-all(f32[16,1,8192]{2,1,0:T(1,128)S(1)} %reshape.427), channel_id=1, replica_groups=mesh['frag'=8,'grid'=16] {'grid'}, dimensions={0} | all-to-all | bytes 1048576 | tf_op jit(solution)/shard_map/all_to_all | solution.py:99
  206.2 7.6 %all-to-all-done.6 = f32[16,2,256]{2,1,0:T(2,128)S(1)} async-done(((f32[16,2,256]{2,1,0:T(2,128)}), f32[16,2,256]{2,1,0:T(2,128)S(1)}, u32[]{:S(2)}, u32[]{:S(2)}) %all-to-all-start.6) | async-done | bytes 32800 | tf_op jit(solution)/shard_map/all_to_all | solution.py:134
  214.1 92.4 %while.47 = (s32[]{:T(128)}, bf16[2,1024,128]{1,2,0:T(8,128)(2,1)S(1)}, s32[2]{0:T(128)S(1)}, bf16[2,1024,1024]{2,1,0:T(8,128)(2,1)}, bf16[2,1024,128]{1,2,0:T(8...) while((s32[]{:T(128)}, ...), condition=%wide.region_9.12_spmd, body=%wide.region_8.11_spmd.sunk | while | flops 3090301184 | bytes 30052988 | solution.py:161
  214.8 7.6 %fusion.358 = f32[1024,128]{1,0:T(8,128)S(1)} fusion(bf16[2,2048,1024]{2,1,0:T(8,128)(2,1)} %get-tuple-element.629, s32[]{:T(128)} %get-tuple-element.615, f32[2048]{0:T(1024)S(1)} %bitcast.379, bf16[1,1024,128]{2,1,0:T(8,128)(2,1)S(1)} %copy.111), kind=kOutput, calls=%fused_computation.46.clone.1 | convolution fusion | flops 1074266112 | bytes 9184256 | tf_op jit(solution)/shard_map/while/body/eval_jaxpr/dot_general | solution.py:36
  237.0 11.7 %cholesky.194 = f32[128,128]{1,0:T(8,128)S(1)} custom-call(f32[128,128]{1,0:T(8,128)S(1)} %fusion.363), custom_call_target="Cholesky" | custom-call | tf_op jit(solution)/shard_map/while/body/eval_jaxpr/jit(cholesky)/cholesky | solution.py:28
  250.0 9.8 %custom-call.14 = f32[1,128,128]{1,2,0:T(8,128)S(1)} custom-call(f32[1,128,128]{2,1,0:T(8,128)S(1)} %fusion.364), custom_call_target="InvertDiagBlocksLowerTriangular" | custom-call | tf_op jit(solution)/shard_map/while/body/eval_jaxpr/jit(_solve_triangular)/triangular_solve | solution.py:29
  283.0 11.7 %cholesky.194 = f32[128,128]{1,0:T(8,128)S(1)} custom-call(f32[128,128]{1,0:T(8,128)S(1)} %fusion.363), custom_call_target="Cholesky" | custom-call | tf_op jit(solution)/shard_map/while/body/eval_jaxpr/jit(cholesky)/cholesky | solution.py:28
  296.1 9.8 %custom-call.14 = f32[1,128,128]{1,2,0:T(8,128)S(1)} custom-call(f32[1,128,128]{2,1,0:T(8,128)S(1)} %fusion.364), custom_call_target="InvertDiagBlocksLowerTriangular" | custom-call | tf_op jit(solution)/shard_map/while/body/eval_jaxpr/jit(_solve_triangular)/triangular_solve | solution.py:29
  306.6 92.2 %while.48 = (s32[]{:T(128)}, bf16[2,1024,128]{1,2,0:T(8,128)(2,1)S(1)}, s32[2]{0:T(128)S(1)}, bf16[2,1024,1024]{2,1,0:T(8,128)(2,1)}, bf16[2,1024,128]{1,2,0:T(8...) while((s32[]{:T(128)}, ...), condition=%wide.region_11.14_spmd, body=%wide.region_10.13_spmd.sunk | while | flops 3090301184 | bytes 30052988 | solution.py:161
  329.2 11.7 %cholesky.206 = f32[128,128]{1,0:T(8,128)S(1)} custom-call(f32[128,128]{1,0:T(8,128)S(1)} %fusion.385), custom_call_target="Cholesky" | custom-call | tf_op jit(solution)/shard_map/while/body/eval_jaxpr/jit(cholesky)/cholesky | solution.py:28
  342.3 9.8 %custom-call.15 = f32[1,128,128]{1,2,0:T(8,128)S(1)} custom-call(f32[1,128,128]{2,1,0:T(8,128)S(1)} %fusion.386), custom_call_target="InvertDiagBlocksLowerTriangular" | custom-call | tf_op jit(solution)/shard_map/while/body/eval_jaxpr/jit(_solve_triangular)/triangular_solve | solution.py:29
  375.3 11.7 %cholesky.206 = f32[128,128]{1,0:T(8,128)S(1)} custom-call(f32[128,128]{1,0:T(8,128)S(1)} %fusion.385), custom_call_target="Cholesky" | custom-call | tf_op jit(solution)/shard_map/while/body/eval_jaxpr/jit(cholesky)/cholesky | solution.py:28
  388.3 9.8 %custom-call.15 = f32[1,128,128]{1,2,0:T(8,128)S(1)} custom-call(f32[1,128,128]{2,1,0:T(8,128)S(1)} %fusion.386), custom_call_target="InvertDiagBlocksLowerTriangular" | custom-call | tf_op jit(solution)/shard_map/while/body/eval_jaxpr/jit(_solve_triangular)/triangular_solve | solution.py:29
  398.8 8.2 %while.49 = (s32[]{:T(128)}, f32[2,2048]{1,0:T(2,128)S(1)}, bf16[2,2048,1024]{2,1,0:T(8,128)(2,1)}, bf16[2,1024,128]{1,2,0:T(8,128)(2,1)S(1)}, f32[2,2048]{1,0:T(2,128)S(1)}, /*index=5*/s32[]{:T(128)}, s32[]{:T(128)}) while((s32[]{:T(128)}, f32[2,2048]{1,0:T(2,128)S(1)}, bf16[2,2048,1024]{2,1,0:T(8,128)(2,1)}, ...), condition=%wide.region_14.17_spmd, body=%wide.region_12.16_spmd.sunk | while | flops 537397248 | bytes 5571161 | solution.py:162
  407.2 10.7 %all_to_all.109 = f32[16,2,256]{2,1,0:T(2,128)S(1)} all-to-all(f32[16,2,256]{2,1,0:T(2,128)S(1)} %copy.92), channel_id=1, replica_groups=mesh['frag'=8,'grid'=16] {'grid'}, dimensions={0} | all-to-all | bytes 65536 | tf_op jit(solution)/shard_map/all_to_all | solution.py:134
  (185 shorter events, 197.8 us)
Async XLA Ops:
  3.2 74.1 %all-to-all-start = ((s32[16,2,1]{1,2,0:T(1,128)}), s32[16,2,1]{1,2,0:T(1,128)S(1)}, u32[]{:S(2)}, u32[]{:S(2)}) async-start(s32[16,2,1]{1,2,0:T(1,128)} %bitcast.37), calls=%async_computation | async-start | bytes 16384 | tf_op jit(solution)/shard_map/all_to_all | solution.py:135
  11.5 80.9 %copy-start.1 = (f32[32,16,256]{2,1,0:T(8,128)S(1)}, f32[32,16,256]{2,1,0:T(8,128)}, u32[]{:S(2)}) copy-start(f32[32,16,256]{2,1,0:T(8,128)} %param.21) | copy-start | bytes 1572868
  37.6 4.4 %copy-start.2 = (s32[2]{0:T(128)S(1)}, s32[2]{0:T(128)}, u32[]{:S(2)}) copy-start(s32[2]{0:T(128)} %get-tuple-element.602) | copy-start | bytes 28 | tf_op jit(solution)/shard_map/while
  70.0 4.4 %copy-start.2 = (s32[2]{0:T(128)S(1)}, s32[2]{0:T(128)}, u32[]{:S(2)}) copy-start(s32[2]{0:T(128)} %get-tuple-element.602) | copy-start | bytes 28 | tf_op jit(solution)/shard_map/while
  77.3 15.0 %all-to-all-start.1 = ((f32[16,2,256]{2,1,0:T(2,128)}), f32[16,2,256]{2,1,0:T(2,128)S(1)}, u32[]{:S(2)}, u32[]{:S(2)}) async-start(f32[16,2,256]{2,1,0:T(2,128)} %copy.77), calls=%async_computation.1 | async-start | bytes 65536 | tf_op jit(solution)/shard_map/all_to_all | solution.py:134
  122.7 15.0 %all-to-all-start.3 = ((f32[8,1,16384]{2,1,0:T(1,128)}), f32[8,1,16384]{2,1,0:T(1,128)S(1)}, u32[]{:S(2)}, u32[]{:S(2)}) async-start(f32[8,1,16384]{2,1,0:T(1,128)} %reshape.423), calls=%async_computation.3 | async-start | bytes 1048576 | tf_op jit(solution)/shard_map/all_to_all | solution.py:86
  196.5 17.6 %copy-start.3 = (s32[2]{0:T(128)S(1)}, s32[2]{0:T(128)}, u32[]{:S(2)}) copy-start(s32[2]{0:T(128)} %param.24) | copy-start | bytes 28
  201.7 12.5 %copy-start = (f32[512,256]{1,0:T(8,128)}, f32[512,256]{1,0:T(8,128)S(1)}, u32[]{:S(2)}) copy-start(f32[512,256]{1,0:T(8,128)S(1)} %fusion.223) | copy-start | bytes 1572868
  202.7 11.1 %all-to-all-start.6 = ((f32[16,2,256]{2,1,0:T(2,128)}), f32[16,2,256]{2,1,0:T(2,128)S(1)}, u32[]{:S(2)}, u32[]{:S(2)}) async-start(f32[16,2,256]{2,1,0:T(2,128)} %all_to_all.93), calls=%async_computation.6 | async-start | bytes 65536 | tf_op jit(solution)/shard_map/all_to_all | solution.py:134
where the time goes:
time: 427 us; the launch traced here: 419 us
  other arithmetic  148 us (35%)
  matrix products  119 us (28%)
  blocking collectives  51.3 us (12%)
  local copies, waits for them, and re-layouts  44.8 us (10%)
  waiting for transfers between devices  24 us (6%)
  starting transfers between devices  23.8 us (6%)
  loops' own time  6.46 us (2%)
    another operation x18, other arithmetic, orthonormalize(): factor = jnp.linalg.cholesky(gram)  74.5 us
    another operation x12, other arithmetic, orthonormalize(): return jax.scipy.linalg.solve_triangular(factor, block.T, lower=True).T  62.9 us
    dot_general x8, matrix products, apply_hamiltonian(): lax.dot_general(basis_f, weighted, (((0,), (0,)), ((), ())), preferred_el...  60.8 us
    dot_general x8, matrix products, apply_hamiltonian(): local_part = jnp.dot(kinetic_f, vector, preferred_element_type=jnp.float32)  18.5 us
    dot_general x4, matrix products, density_rows(): jnp.dot(basis_f, orbitals.astype(jnp.bfloat16), preferred_element_type=jn...  14.9 us
    all_to_all x1, blocking collectives, spectral(): lax.all_to_all(rows_back, 'grid', split_axis=1, concat_axis=2, tiled=True)  14.4 us
    all_to_all x2, waiting for transfers between devices, tile_trade(): lax.all_to_all(values, 'grid', split_axis=0, concat_axis=0, tiled=True)  13.9 us
    all_to_all x1, blocking collectives, spectral(): lax.all_to_all(spectrum, 'grid', split_axis=2, concat_axis=1, tiled=True)  13.2 us
  transfers between devices with their start and end apart: 4, of which 3 were waited for; matrix products, arithmetic and copies ran while one was open for 15% of the time, Pallas kernels for 0%

commit v1 on v0

v1 whole, which is shorter than its diff:
```python
import jax
import jax.numpy as jnp
import ml_dtypes
import numpy as np
from jax import lax
from jax.experimental import pallas as pl
from jax.experimental.pallas import tpu as pltpu
from jax.sharding import PartitionSpec as P

f32 = jnp.float32
bf16 = jnp.bfloat16

STEPS = 2
CENTER = 5.0
HALF = 4.0
FRAGS = 2
TILES = 8
ENTRIES = FRAGS * TILES
N = 256
GROUPS = 8
OWNERS = 16
PEERS = GROUPS * OWNERS
PLANES = N // GROUPS
ROWS = N // OWNERS
CELLS = PLANES * ROWS
ORB = 128
BASIS = 1024
POINTS = TILES * N
MSG = 9
BOTH = ("frag", "grid")

NN = (((1,), (0,)), ((), ()))
NT = (((1,), (1,)), ((), ()))
TN = (((0,), (0,)), ((), ()))


def sine_table():
    index = np.arange(1, N + 1)
    phase = np.outer(index, index) % (2 * (N + 1))
    return np.sqrt(2.0 / (N + 1)) * np.sin(np.pi * phase / (N + 1))


def eigen_values():
    return 4.0 * np.sin(np.pi * np.arange(1, N + 1) / (2.0 * (N + 1))) ** 2


def halves(table):
    table = table.astype(np.float32)
    high = table.astype(ml_dtypes.bfloat16)
    low = (table - high.astype(np.float32)).astype(ml_dtypes.bfloat16)
    return jnp.asarray(np.stack([high, low]))


def dot(a, b, dims=NN):
    return lax.dot_general(a, b, dims, preferred_element_type=f32)


def split(x):
    high = x.astype(bf16)
    return high, (x - high.astype(f32)).astype(bf16)


def split3(x):
    high = x.astype(bf16)
    rest = x - high.astype(f32)
    middle = rest.astype(bf16)
    return high, middle, (rest - middle.astype(f32)).astype(bf16)


def dot3(a, b, dims=NN):
    return dot(a[0], b[0], dims) + (dot(a[0], b[1], dims) + dot(a[1], b[0], dims))


def spread(x):
    return jnp.broadcast_to(x, (8, 128))


def tree_sum(terms):
    terms = list(terms)
    while len(terms) > 1:
        terms = [
            terms[i] + terms[i + 1] if i + 1 < len(terms) else terms[i]
            for i in range(0, len(terms), 2)
        ]
    return terms[0]


def eliminate(panel, k, lane, sub):
    inside = (lane >= k) & (lane < k + 8)
    column = [spread(panel[:, k + j : k + j + 1]) for j in range(8)]
    panel = jnp.where(inside, jnp.where(lane - k == sub, 1.0, 0.0), panel)
    factor = jnp.zeros((8, 128), f32)
    scale = jnp.zeros((8, 128), f32)
    for j in range(8):
        pivot = spread(column[j][j : j + 1, :])
        guess = pl.reciprocal(pivot, approx=True)
        inverse = guess * (2.0 - pivot * guess)
        row = spread(panel[j : j + 1, :])
        factor = jnp.where(sub == j, row * lax.rsqrt(pivot), factor)
        scale = jnp.where(sub == j, inverse, scale)
        ratio = jnp.where(sub == j, 0.0, column[j] * inverse)
        for i in range(j + 1, 8):
            column[i] = column[i] - ratio * spread(column[i][j : j + 1, :])
        panel = panel - ratio * row
    return jnp.where(lane < k + 8, factor, 0.0), panel * scale, inside


def inverse_factors(gram, factors):
    lane = lax.broadcasted_iota(jnp.int32, (8, 128), 1)
    sub = lax.broadcasted_iota(jnp.int32, (8, 128), 0)
    for block in range(ORB // 8):
        k = 8 * block
        for f in range(FRAGS):
            rows, solved, inside = eliminate(gram[f, k : k + 8, :], k, lane, sub)
            factors[f, k : k + 8, :] = rows
            solved_rows = [spread(solved[j : j + 1, :]) for j in range(8)]
            for q in range(block + 1, ORB // 8):
                below = gram[f, 8 * q : 8 * q + 8, :]
                update = tree_sum(
                    [spread(below[:, k + j : k + j + 1]) * solved_rows[j] for j in range(8)]
                )
                gram[f, 8 * q : 8 * q + 8, :] = jnp.where(inside, 0.0, below) - update


def line_index(ids, counts, e):
    f, t = divmod(e, TILES)
    return jnp.where(t < counts[f], ids[f, t], -1)


def live_rows(counts, f):
    slot = lax.broadcasted_iota(jnp.int32, (TILES, N), 0)
    return (slot < counts[f]).astype(f32)


def density_lines(values, lines, f):
    row = 2.0 * jnp.sum(values * values, axis=0, keepdims=True)
    for t in range(TILES):
        lines[f * TILES + t : f * TILES + t + 1, :] = row[:, t * N : (t + 1) * N]


def start_kernel(
    ids, counts, start, ground, table_z, basis, send, orbitals, collocated,
    held, sem, gram, factors, ground_high, ground_low, lines,
):
    copies = [pltpu.make_async_copy(basis.at[f], held.at[f], sem.at[f]) for f in range(FRAGS)]
    for copy in copies:
        copy.start()
    eye = (
        lax.broadcasted_iota(jnp.int32, (ORB, ORB), 0)
        == lax.broadcasted_iota(jnp.int32, (ORB, ORB), 1)
    ).astype(f32).astype(bf16)
    turned = []
    for f in range(FRAGS):
        across = dot(eye, start[f], NT).astype(bf16)
        turned.append(across)
        gram[f] = dot(across, across, NT)
    for y in range(ROWS):
        high, low = split(ground[:, y, :])
        ground_high[y * PLANES : (y + 1) * PLANES, :] = high
        ground_low[y * PLANES : (y + 1) * PLANES, :] = low
    table = (table_z[0], table_z[1])
    spectrum = dot3(table, (ground_high[...], ground_low[...]), NT)
    for z in range(2):
        for g in range(4):
            send[pl.ds(z * 4 + g, PEERS, stride=MSG), :] = spectrum[
                z * PEERS : (z + 1) * PEERS, g * 128 : (g + 1) * 128
            ]
    inverse_factors(gram, factors)
    charges = []
    for f in range(FRAGS):
        parts = split3(factors[f])
        rotated = dot(parts[0], turned[f]) + (dot(parts[1], turned[f]) + dot(parts[2], turned[f]))
        rounded = rotated.astype(bf16)
        orbitals[f] = rounded
        copies[f].wait()
        values = dot(rounded, held[f], NT)
        collocated[f] = values
        density_lines(values, lines, f)
        live = live_rows(counts, f)
        density = lines[f * TILES : (f + 1) * TILES, :] * live
        mean = jnp.sum(density) / (counts[f] * N).astype(f32)
        charges.append((density - mean) * live)
    charge = jnp.concatenate(charges, axis=0)
    blank = jnp.zeros((ENTRIES, N), f32)
    message = jnp.zeros((PEERS, 128), f32)
    for z in range(2):
        padded = jnp.concatenate([charge if i == z else blank for i in range(8)], axis=0)
        rows = slice(z * PEERS, (z + 1) * PEERS)
        message = message + dot3((table_z[0, rows, :], table_z[1, rows, :]), split(padded), NT)
    lane = lax.broadcasted_iota(jnp.int32, (1, 128), 1)
    label = jnp.zeros((1, 128), f32)
    for e in range(ENTRIES):
        label = jnp.where(lane == 2 * ENTRIES + e, line_index(ids, counts, e).astype(f32), label)
    send[pl.ds(8, PEERS, stride=MSG), :] = message + label


def exchange_chunks(parts):
    chunk = lax.broadcasted_iota(jnp.int32, (8, 128), 1) >> 5
    results = []
    for j in range(4):
        total = None
        for i in range(4):
            moved = parts[i] if i == j else pltpu.roll(parts[i], ((i - j) % 4) * 32, 1)
            total = moved if total is None else jnp.where(chunk == i, moved, total)
        results.append(total)
    return results


def solve_kernel(
    arrived, table, table_y, table_yt, eigen, eigen_z, send, plane, wanted_x, placed,
):
    labels = arrived[pl.ds(8, PEERS, stride=MSG), :]
    turned = labels.T
    index = labels.astype(jnp.int32)
    index_t = turned.astype(jnp.int32)
    plane_x = index >> 8
    cell_y = index_t & 255
    row_y = ((cell_y & 15) << 4) + (cell_y >> 4)
    lane = lax.broadcasted_iota(jnp.int32, (PEERS, N), 1)
    sub = lax.broadcasted_iota(jnp.int32, (N, PEERS), 0)
    for e in range(ENTRIES):
        line = 2 * ENTRIES + e
        wanted_x[e * PEERS : (e + 1) * PEERS, :] = (
            (plane_x[:, line : line + 1] == lane).astype(f32).astype(bf16)
        )
        here = row_y[line : line + 1, :] == sub
        for z in range(2):
            value = turned[z * ENTRIES + e : z * ENTRIES + e + 1, :]
            high = value.astype(bf16).astype(f32)
            for part, piece in enumerate((high, value - high)):
                placed[
                    (2 * z + part) * N : (2 * z + part + 1) * N, e * PEERS : (e + 1) * PEERS
                ] = jnp.where(here, piece, 0.0).astype(bf16)
    gathered = dot(placed[...], wanted_x[...])
    for z in range(2):
        for hi in range(2):
            for half in range(2):
                for g in range(4):
                    base = (hi * 4 * OWNERS + half * 8) * MSG + z * 4 + g
                    parts = exchange_chunks(
                        [
                            arrived[pl.ds(base + i * OWNERS * MSG, 8, stride=MSG), :]
                            for i in range(4)
                        ]
                    )
                    for i in range(4):
                        row = z * N + (g * 4 + i) * OWNERS + half * 8
                        plane[row : row + 8, hi * 128 : (hi + 1) * 128] = parts[i]
    table_x = (table[0], table[1])
    forward = (table_y[0], table_y[1])
    backward = (table_yt[0], table_yt[1])
    source = jnp.concatenate(
        [
            gathered[2 * z * N : (2 * z + 1) * N]
            + gathered[(2 * z + 1) * N : (2 * z + 2) * N]
            - plane[z * N : (z + 1) * N, :]
            for z in range(2)
        ],
        axis=0,
    )
    along_x = dot3(split(source), table_x)
    for z in range(2):
        modes = dot3(forward, split(along_x[z * N : (z + 1) * N]))
        modes = modes / (eigen[...] + eigen_z[z])
        plane[z * N : (z + 1) * N, :] = dot3(backward, split(modes))
    plane[...] = dot3(split(plane[...]), table_x)
    for z in range(2):
        for hi in range(2):
            for half in range(2):
                for g in range(4):
                    base = (hi * 4 * OWNERS + half * 8) * MSG + z * 4 + g
                    parts = []
                    for i in range(4):
                        row = z * N + (g * 4 + i) * OWNERS + half * 8
                        parts.append(plane[row : row + 8, hi * 128 : (hi + 1) * 128])
                    parts = exchange_chunks(parts)
                    for i in range(4):
                        send[pl.ds(base + i * OWNERS * MSG, 8, stride=MSG), :] = parts[i]
    high, low = split(plane[...])
    stacked = jnp.concatenate([high, low], axis=0)
    found = [[], []]
    for e in range(ENTRIES):
        line = 2 * ENTRIES + e
        here = row_y[line : line + 1, :] == sub
        columns = dot(stacked, wanted_x[e * PEERS : (e + 1) * PEERS, :], NT)
        for z in range(2):
            both = columns[z * N : (z + 1) * N] + columns[(2 + z) * N : (3 + z) * N]
            found[z].append(jnp.sum(jnp.where(here, both, 0.0), axis=0, keepdims=True))
    rows = jnp.concatenate(
        found[0] + found[1] + [jnp.zeros((PEERS - 2 * ENTRIES, PEERS), f32)], axis=0
    )
    send[pl.ds(8, PEERS, stride=MSG), :] = rows.T


def cycle_kernel(
    ids, counts, degrees, arrived, table_z, first, first_collocated, basis, kinetic, send,
    held, held_kinetic, sem, field, orbitals, collocated, following, gram, factors, lines,
):
    copies = []
    for f in range(FRAGS):
        for i, (source, target) in enumerate(((basis, held), (kinetic, held_kinetic))):
            copies.append(
                pltpu.make_async_copy(source.at[f], target.at[f], sem.at[2 * f + i])
            )
    for copy in copies:
        copy.start()
    turned = arrived[pl.ds(8, PEERS, stride=MSG), :].T
    values = jnp.zeros((ENTRIES, N), f32)
    for z in range(2):
        rows = slice(z * PEERS, (z + 1) * PEERS)
        values = values + dot3(
            split(turned[z * ENTRIES : (z + 1) * ENTRIES, :]),
            (table_z[0, rows, :], table_z[1, rows, :]),
        )
    for f in range(FRAGS):
        field[f * TILES : (f + 1) * TILES, :] = (
            values[f * TILES : (f + 1) * TILES] * live_rows(counts, f)
        )
    for f in range(FRAGS):
        orbitals[f] = first[f]
        collocated[f] = first_collocated[f]
    for copy in copies:
        copy.wait()

    def apply(f, vector, points):
        weights = jnp.concatenate(
            [field[f * TILES + t : f * TILES + t + 1, :] for t in range(TILES)], axis=1
        )
        weighted = (points * weights).astype(bf16)
        return dot(vector, held_kinetic[f]) + dot(weighted, held[f])

    def step(_, carry):
        for f in range(FRAGS):
            earlier = orbitals[f]
            current = (apply(f, earlier, collocated[f]) - CENTER * earlier.astype(f32)) / HALF
            rounded = current.astype(bf16)
            points = dot(rounded, held[f], NT)
            second = 2.0 * (
                apply(f, rounded, points) - CENTER * rounded.astype(f32)
            ) / HALF - earlier.astype(f32)
            chosen = jnp.where(degrees[f] == 2, second, current)
            following[f] = chosen
            gram[f] = lax.dot_general(
                chosen, chosen, NT, precision=lax.Precision.HIGHEST, preferred_element_type=f32
            )
        inverse_factors(gram, factors)
        for f in range(FRAGS):
            rotated = lax.dot_general(
                factors[f], following[f], NN,
                precision=lax.Precision.HIGHEST, preferred_element_type=f32,
            )
            rounded = rotated.astype(bf16)
            orbitals[f] = rounded
            collocated[f] = dot(rounded, held[f], NT)
        return carry

    lax.fori_loop(0, STEPS, step, 0)
    for f in range(FRAGS):
        density_lines(collocated[f], lines, f)
    send[...] = jnp.full((OWNERS * 8, 128), -1.0, f32)
    line_of = [line_index(ids, counts, e) for e in range(ENTRIES)]
    owner_of = [jnp.where(line >= 0, (line & (N - 1)) >> 4, -1) for line in line_of]
    for e in range(ENTRIES):
        rank = jnp.int32(0)
        for i in range(e):
            rank = rank + jnp.where(owner_of[i] == owner_of[e], 1, 0)
        rank = jnp.minimum(rank, 1)
        local = ((line_of[e] >> 8) & (PLANES - 1)) * ROWS + (line_of[e] & (ROWS - 1))

        @pl.when(line_of[e] >= 0)
        def _():
            base = owner_of[e] * 8
            for half in range(2):
                send[pl.ds(base + rank * 2 + half, 1), :] = lines[
                    e : e + 1, half * 128 : (half + 1) * 128
                ]
            send[pl.ds(base + 4 + rank, 1), :] = jnp.full((1, 128), local.astype(f32))


def potential_kernel(arrived, table_z, potential, modes):
    for z in range(2):
        for g in range(4):
            modes[z * PEERS : (z + 1) * PEERS, g * 128 : (g + 1) * 128] = arrived[
                pl.ds(z * 4 + g, PEERS, stride=MSG), :
            ]
    values = dot3(split(modes[...]), (table_z[0], table_z[1]), TN)
    for y in range(ROWS):
        potential[:, y, :] = values[y * PLANES : (y + 1) * PLANES]


def density_kernel(arrived, density):
    lane = lax.broadcasted_iota(jnp.int32, (OWNERS, CELLS), 1)
    masks, values = [], []
    for slot in range(2):
        index = arrived[pl.ds(4 + slot, OWNERS, stride=8), :].astype(jnp.int32)
        masks.append(
            (jnp.concatenate([index] * (CELLS // 128), axis=1) == lane).astype(f32)
        )
        values.append(
            jnp.concatenate(
                [arrived[pl.ds(slot * 2 + half, OWNERS, stride=8), :] for half in range(2)],
                axis=1,
            )
        )
    mask = jnp.concatenate(masks, axis=0).astype(bf16)
    parts = split3(jnp.concatenate(values, axis=0))
    density[...] = dot(mask, parts[0], TN) + (dot(mask, parts[1], TN) + dot(mask, parts[2], TN))


VM = pl.BlockSpec(memory_space=pltpu.VMEM)
SM = pl.BlockSpec(memory_space=pltpu.SMEM)
ANY = pl.BlockSpec(memory_space=pl.ANY)


def call(kernel, name, in_specs, shapes, scratch, operands, flops=0, limit=40):
    outs = [jax.ShapeDtypeStruct(shape, dtype) for shape, dtype in shapes]
    single = len(outs) == 1
    return pl.pallas_call(
        kernel,
        out_shape=outs[0] if single else outs,
        in_specs=in_specs,
        out_specs=VM if single else [VM] * len(outs),
        scratch_shapes=scratch,
        name=name,
        cost_estimate=pl.CostEstimate(flops=flops, bytes_accessed=1 << 20, transcendentals=0),
        compiler_params=pltpu.CompilerParams(vmem_limit_bytes=limit << 20),
    )(*operands)


def trade(message):
    packed = message.reshape(PEERS, MSG, 1, 128)
    return lax.all_to_all(packed, BOTH, 0, 0, tiled=True).reshape(PEERS * MSG, 128)


def shards(kinetic, basis, start_orbitals, background, tile_ids, tile_counts, degrees):
    sines = sine_table()
    eigen = eigen_values()
    order_z = np.concatenate([np.arange(0, N, 2), np.arange(1, N, 2)])
    row = np.arange(N)
    order_y = (row % OWNERS) * ROWS + row // OWNERS
    table_z = halves(sines[order_z])
    table_x = halves(sines)
    table_y = halves(sines[:, order_y])
    table_yt = halves(sines[order_y, :])
    eigen_xy = jnp.asarray((eigen[:, None] + eigen[None, :]).astype(np.float32))
    device = lax.axis_index("frag") * OWNERS + lax.axis_index("grid")
    eigen_z = lax.dynamic_slice(jnp.asarray(eigen.astype(np.float32)), (2 * device,), (2,))

    dma = pltpu.SemaphoreType.DMA
    message_a, first, collocated = call(
        start_kernel, "start",
        [SM, SM, VM, VM, VM, ANY],
        [
            ((PEERS * MSG, 128), f32),
            ((FRAGS, ORB, BASIS), bf16),
            ((FRAGS, ORB, POINTS), f32),
        ],
        [
            pltpu.VMEM((FRAGS, POINTS, BASIS), bf16),
            dma((FRAGS,)),
            pltpu.VMEM((FRAGS, ORB, ORB), f32),
            pltpu.VMEM((FRAGS, ORB, ORB), f32),
            pltpu.VMEM((CELLS, N), bf16),
            pltpu.VMEM((CELLS, N), bf16),
            pltpu.VMEM((ENTRIES, N), f32),
        ],
        (tile_ids, tile_counts, start_orbitals, background, table_z, basis),
        flops=10**10,
    )
    arrived_a = trade(message_a)
    message_b = call(
        solve_kernel, "solve",
        [VM, VM, VM, VM, VM, SM],
        [((PEERS * MSG, 128), f32)],
        [
            pltpu.VMEM((2 * N, N), f32),
            pltpu.VMEM((PEERS * ENTRIES, N), bf16),
            pltpu.VMEM((4 * N, PEERS * ENTRIES), bf16),
        ],
        (arrived_a, table_x, table_y, table_yt, eigen_xy, eigen_z),
        flops=5 * 10**9,
    )
    arrived_b = trade(message_b)
    message_c = call(
        cycle_kernel, "cycle",
        [SM, SM, SM, VM, VM, VM, VM, ANY, ANY],
        [((OWNERS * 8, 128), f32)],
        [
            pltpu.VMEM((FRAGS, POINTS, BASIS), bf16),
            pltpu.VMEM((FRAGS, BASIS, BASIS), bf16),
            dma((2 * FRAGS,)),
            pltpu.VMEM((ENTRIES, N), f32),
            pltpu.VMEM((FRAGS, ORB, BASIS), bf16),
            pltpu.VMEM((FRAGS, ORB, POINTS), f32),
            pltpu.VMEM((FRAGS, ORB, BASIS), f32),
            pltpu.VMEM((FRAGS, ORB, ORB), f32),
            pltpu.VMEM((FRAGS, ORB, ORB), f32),
            pltpu.VMEM((ENTRIES, N), f32),
        ],
        (
            tile_ids, tile_counts, degrees, arrived_b, table_z, first, collocated, basis, kinetic,
        ),
        flops=4 * 10**10,
    )
    arrived_c = lax.all_to_all(
        message_c.reshape(OWNERS, 8, 128), "grid", 0, 0, tiled=True
    ).reshape(OWNERS * 8, 128)
    potential = call(
        potential_kernel, "potential", [VM, VM], [((PLANES, ROWS, N), f32)],
        [pltpu.VMEM((2 * PEERS, CELLS), f32)], (arrived_b, table_z), flops=10**9,
    )
    density = call(
        density_kernel, "density", [VM], [((CELLS, N), f32)], [], (arrived_c,), flops=10**8,
    )
    return potential, density.reshape(PLANES, ROWS, N)


def solution(mesh):
    in_specs = (
        P(BOTH, None, None),
        P(BOTH, None, None),
        P(BOTH, None, None),
        P("frag", "grid", None),
        P(BOTH, None),
        P(BOTH),
        P(BOTH),
    )
    out_specs = (P("frag", "grid", None), P("frag", "grid", None))
    return jax.shard_map(shards, mesh=mesh, in_specs=in_specs, out_specs=out_specs, check_vma=False)
```

time: 427 us -> 127 us (0.30); the launches traced: 419 us -> 126 us
  other arithmetic: 148 us -> 0 us
  matrix products: 119 us -> 0 us
  Pallas kernels: 0 us -> 62.7 us
  local copies, waits for them, and re-layouts: 44.8 us -> 9.2 us
  blocking collectives: 51.3 us -> 18.5 us
  starting transfers between devices: 23.8 us -> 14.8 us
  loops' own time: 6.46 us -> 0 us
    another operation x30 -> x0, other arithmetic: 137 us -> none  [the longest x18 74.5 us: orthonormalize(): factor = jnp.linalg.cholesky(gram)]
    dot_general x38 -> x0, matrix products: 114 us -> none  [the longest x8 60.8 us: apply_hamiltonian(): lax.dot_general(basis_f, weighted, (((0,), (0,)), ((), ())), preferred_el...]
    pallas_call x0 -> x5, Pallas kernels: none -> 62.7 us  [call(): pl.pallas_call(kernel, out_shape=outs[0] if single else outs, in_specs=in...]
    all_to_all x4 -> x1, blocking collectives: 51.3 us -> 18.5 us  [trade(): lax.all_to_all(packed, BOTH, 0, 0, tiled=True).reshape(PEERS * MSG, 128)]
    all_to_all x13 -> x0, local copies, waits for them, and re-layouts: 20.3 us -> none  [the longest x3 5.21 us: spectral(): lax.all_to_all(spectrum, 'grid', split_axis=2, concat_axis=1, tiled=True)]
    all_to_all x4 -> x2, starting transfers between devices: 23.8 us -> 14.8 us  [the longest x1 11.3 us: trade(): lax.all_to_all(packed, BOTH, 0, 0, tiled=True).reshape(PEERS * MSG, 128)]
    all_to_all x5 -> x0, other arithmetic: 8.21 us -> none  [the longest x1 1.89 us: spectral(): lax.all_to_all(rows_back, 'grid', split_axis=1, concat_axis=2, tiled=True)]
    another operation x4 -> x0, loops' own time: 6.46 us -> none  [the longest x2 3.62 us: shards(): orbitals = lax.map(filter_step, (kinetic, basis, field, degrees, orbitals))]
  transfers between devices with their start and end apart: 4 -> 2, of which waited for: 3 -> 2; matrix products, arithmetic and copies ran while one was open for 15% -> 0% of each run, Pallas kernels for 0% -> 1%
where the time goes in v1:
time: 127 us; the launch traced here: 126 us
  Pallas kernels  62.7 us (49%)
  waiting for transfers between devices  20.3 us (16%)
  blocking collectives  18.5 us (15%)
  starting transfers between devices  14.8 us (12%)
  local copies, waits for them, and re-layouts  9.2 us (7%)
    pallas_call x5, Pallas kernels, call(): pl.pallas_call(kernel, out_shape=outs[0] if single else outs, in_specs=in...  62.7 us
    all_to_all x1, blocking collectives, trade(): lax.all_to_all(packed, BOTH, 0, 0, tiled=True).reshape(PEERS * MSG, 128)  18.5 us
    all_to_all x1, waiting for transfers between devices, trade(): lax.all_to_all(packed, BOTH, 0, 0, tiled=True).reshape(PEERS * MSG, 128)  14 us
    all_to_all x1, starting transfers between devices, trade(): lax.all_to_all(packed, BOTH, 0, 0, tiled=True).reshape(PEERS * MSG, 128)  11.3 us
    unnamed x36, local copies, waits for them, and re-layouts  9.12 us
    all_to_all x1, waiting for transfers between devices, shards(): lax.all_to_all(message_c.reshape(OWNERS, 8, 128), 'grid', 0, 0, tiled=True)  6.26 us
    all_to_all x1, starting transfers between devices, shards(): lax.all_to_all(message_c.reshape(OWNERS, 8, 128), 'grid', 0, 0, tiled=True)  3.51 us
  transfers between devices with their start and end apart: 2, of which 2 were waited for; matrix products, arithmetic and copies ran while one was open for 0% of the time, Pallas kernels for 1%

profile of v1, /device:TPU:0, one launch (start us, length us, event | category | flops | bytes accessed | tf_op | source)
XLA Modules:
  0.0 126.3 jit_solution(2384727533066610857)
XLA Ops:
  0.6 0.0 copy-start.17
  0.6 0.0 copy-start
  0.7 3.4 %copy-done = bf16[2,2048,1024]{2,1,0:T(8,128)(2,1)S(1)} copy-done((bf16[2,2048,1024]{2,1,0:T(8,128)(2,1)S(1)}, bf16[2,2048,1024]{2,1,0:T(8,128)(2,1)}, u32[]{:S(2)}) %copy-start) | copy-done | bytes 8388632
  4.0 1.0 copy-done.2
  5.1 1.0 copy-done.3
  6.1 0.7 copy-done.4
  6.8 0.7 copy-done.6
  7.5 0.9 copy-done.9
  8.4 14.6 %start.2 = (f32[1152,128]{1,0:T(8,128)}, bf16[2,128,1024]{2,1,0:T(8,128)(2,1)S(1)}, f32[2,128,2048]{2,1,0:T(8,128)S(1)}) custom-call(s32[2,8]{1,0:T(2,128)S(1)} %copy-done.4, s32[2]{0:T(128)S(1)} %copy-done.6, bf16[2,1024,128]{2,1,0:T(8,128)(2,1)S(1)} %copy-done.2, f32[32,16,256]{2,1,0:T(8,128)S(1)} %copy-done.3, bf16[2,256,256]{2,1,0:T(8,128)(2,1)S(1)} %copy-done.9, ...), custom_call_target="tpu_custom_call" | custom-call | flops 10000000000 | bytes 1048576 | tf_op jit(solution)/shard_map/start/pallas_call | solution.py:418
  23.1 1.3 %copy-done.15 = f32[2,128,2048]{2,1,0:T(8,128)} copy-done((f32[2,128,2048]{2,1,0:T(8,128)}, f32[2,128,2048]{2,1,0:T(8,128)S(1)}, u32[]{:S(2)}) %copy-start.15) | copy-done | bytes 2097176
  24.4 11.3 %all-to-all-start = ((f32[128,9,1,128]{3,2,1,0:T(1,128)}), f32[128,9,1,128]{3,2,1,0:T(1,128)S(1)}, u32[]{:S(2)}, u32[]{:S(2)}) async-start(f32[128,9,1,128]{3,2,1,0:T(1,128)} %bitcast), calls=%async_computation | async-start | bytes 1179648 | tf_op jit(solution)/shard_map/all_to_all | solution.py:432
  35.7 0.1 dynamic_slice.3.eigen_z
  35.8 14.0 %all-to-all-done = f32[128,9,1,128]{3,2,1,0:T(1,128)S(1)} async-done(((f32[128,9,1,128]{3,2,1,0:T(1,128)}), f32[128,9,1,128]{3,2,1,0:T(1,128)S(1)}, u32[]{:S(2)}, u32[]{:S(2)}) %all-to-all-start) | async-done | bytes 589856 | tf_op jit(solution)/shard_map/all_to_all | solution.py:432
  49.8 0.0 copy-start.1
  49.9 0.0 copy-start.5
  49.9 0.0 copy-start.8
  49.9 0.0 copy-start.10
  49.9 7.8 %solve.1 = f32[1152,128]{1,0:T(8,128)S(1)} custom-call(f32[1152,128]{1,0:T(8,128)S(1)} %bitcast.7, bf16[2,256,256]{2,1,0:T(8,128)(2,1)S(1)} %copy-done.11, bf16[2,256,256]{2,1,0:T(8,128)(2,1)S(1)} %copy-done.12, bf16[2,256,256]{2,1,0:T(8,128)(2,1)S(1)} %copy-done.13, f32[256,256]{1,0:T(8,128)S(1)} %copy-done.14, f32[2]{0:T(128)S(1)} %dynamic_slice.3.eigen_z), custom_call_target="tpu_custom_call" | custom-call | flops 5000000000 | bytes 1048576 | tf_op jit(solution)/shard_map/solve/pallas_call | solution.py:418
  57.7 18.5 %all_to_all.15 = f32[128,9,1,128]{3,2,1,0:T(1,128)S(1)} all-to-all(f32[128,9,1,128]{3,2,1,0:T(1,128)S(1)} %bitcast.10), channel_id=1, replica_groups=mesh['frag'=8,'grid'=16] {'frag','grid'}, dimensions={0} | all-to-all | bytes 1179648 | tf_op jit(solution)/shard_map/all_to_all | solution.py:432
  76.2 37.7 %cycle.1 = f32[128,128]{1,0:T(8,128)} custom-call(s32[2,8]{1,0:T(2,128)S(1)} %copy-done.5, s32[2]{0:T(128)S(1)} %copy-done.7, s32[2]{0:T(128)S(1)} %copy-done.8, f32[1152,128]{1,0:T(8,128)S(1)} %bitcast.8, bf16[2,256,256]{2,1,0:T(8,128)(2,1)S(1)} %copy-done.10, bf16[2,128,1024]{2,1,0:T(8,128)(2,1)S(1)} %get-tuple-element.6.first, ...), custom_call_target="tpu_custom_call" | custom-call | flops 40000000000 | bytes 1048576 | tf_op jit(solution)/shard_map/cycle/pallas_call | solution.py:418
  114.0 3.5 %all-to-all-start.2 = ((f32[16,8,128]{2,1,0:T(8,128)}), f32[16,8,128]{2,1,0:T(8,128)S(1)}, u32[]{:S(2)}, u32[]{:S(2)}) async-start(f32[16,8,128]{2,1,0:T(8,128)} %bitcast.4), calls=%async_computation.2 | async-start | bytes 131072 | tf_op jit(solution)/shard_map/all_to_all | solution.py:505
  117.5 1.3 %potential.1 = f32[32,16,256]{2,1,0:T(8,128)} custom-call(f32[1152,128]{1,0:T(8,128)S(1)} %bitcast.9, bf16[2,256,256]{2,1,0:T(8,128)(2,1)S(1)} %copy-done.10), custom_call_target="tpu_custom_call" | custom-call | flops 1000000000 | bytes 1048576 | tf_op jit(solution)/shard_map/potential/pallas_call | solution.py:418
  118.8 6.3 %all-to-all-done.2 = f32[16,8,128]{2,1,0:T(8,128)S(1)} async-done(((f32[16,8,128]{2,1,0:T(8,128)}), f32[16,8,128]{2,1,0:T(8,128)S(1)}, u32[]{:S(2)}, u32[]{:S(2)}) %all-to-all-start.2) | async-done | bytes 65568 | tf_op jit(solution)/shard_map/all_to_all | solution.py:505
  125.1 1.2 density.1
  (23 shorter events, 0.0 us)
Async XLA Ops:
  0.6 35.1 %copy-start.17 = (f32[256]{0:T(256)S(1)}, f32[256]{0:T(256)}, u32[]{:S(2)}) copy-start(f32[256]{0:T(256)} %constant.34.clone) | copy-start | bytes 3076
  0.6 3.4 %copy-start = (bf16[2,2048,1024]{2,1,0:T(8,128)(2,1)S(1)}, bf16[2,2048,1024]{2,1,0:T(8,128)(2,1)}, u32[]{:S(2)}) copy-start(bf16[2,2048,1024]{2,1,0:T(8,128)(2,1)} %basis.3) | copy-start | bytes 25165828
  4.0 1.0 copy-start.2
  5.1 1.0 copy-start.3
  6.1 0.7 copy-start.4
  6.8 0.7 copy-start.6
  7.5 0.9 copy-start.9
  8.4 41.4 %copy-start.11 = (bf16[2,256,256]{2,1,0:T(8,128)(2,1)S(1)}, bf16[2,256,256]{2,1,0:T(8,128)(2,1)}, u32[]{:S(2)}) copy-start(bf16[2,256,256]{2,1,0:T(8,128)(2,1)} %constant.30.clone.table) | copy-start | bytes 786436
  8.4 41.4 %copy-start.12 = (bf16[2,256,256]{2,1,0:T(8,128)(2,1)S(1)}, bf16[2,256,256]{2,1,0:T(8,128)(2,1)}, u32[]{:S(2)}) copy-start(bf16[2,256,256]{2,1,0:T(8,128)(2,1)} %constant.31.clone.table_y) | copy-start | bytes 786436
  8.4 41.4 %copy-start.13 = (bf16[2,256,256]{2,1,0:T(8,128)(2,1)S(1)}, bf16[2,256,256]{2,1,0:T(8,128)(2,1)}, u32[]{:S(2)}) copy-start(bf16[2,256,256]{2,1,0:T(8,128)(2,1)} %constant.32.clone.table_yt) | copy-start | bytes 786436
  8.4 41.4 %copy-start.14 = (f32[256,256]{1,0:T(8,128)S(1)}, f32[256,256]{1,0:T(8,128)}, u32[]{:S(2)}) copy-start(f32[256,256]{1,0:T(8,128)} %constant.33.clone.eigen) | copy-start | bytes 786436
  23.1 1.3 %copy-start.15 = (f32[2,128,2048]{2,1,0:T(8,128)}, f32[2,128,2048]{2,1,0:T(8,128)S(1)}, u32[]{:S(2)}) copy-start(f32[2,128,2048]{2,1,0:T(8,128)S(1)} %get-tuple-element.7.first_collocated) | copy-start | bytes 6291460
  24.4 25.4 %all-to-all-start = ((f32[128,9,1,128]{3,2,1,0:T(1,128)}), f32[128,9,1,128]{3,2,1,0:T(1,128)S(1)}, u32[]{:S(2)}, u32[]{:S(2)}) async-start(f32[128,9,1,128]{3,2,1,0:T(1,128)} %bitcast), calls=%async_computation | async-start | bytes 1179648 | tf_op jit(solution)/shard_map/all_to_all | solution.py:432
  49.8 26.4 %copy-start.1 = (bf16[2,1024,1024]{2,1,0:T(8,128)(2,1)S(1)}, bf16[2,1024,1024]{2,1,0:T(8,128)(2,1)}, u32[]{:S(2)}) copy-start(bf16[2,1024,1024]{2,1,0:T(8,128)(2,1)} %kinetic.1) | copy-start | bytes 12582916
  49.9 26.3 %copy-start.5 = (s32[2,8]{1,0:T(2,128)S(1)}, s32[2,8]{1,0:T(2,128)}, u32[]{:S(2)}) copy-start(s32[2,8]{1,0:T(2,128)} %ids.3) | copy-start | bytes 196
  49.9 26.3 %copy-start.7 = (s32[2]{0:T(128)S(1)}, s32[2]{0:T(128)}, u32[]{:S(2)}) copy-start(s32[2]{0:T(128)} %counts.3) | copy-start | bytes 28
  49.9 26.3 %copy-start.8 = (s32[2]{0:T(128)S(1)}, s32[2]{0:T(128)}, u32[]{:S(2)}) copy-start(s32[2]{0:T(128)} %degrees.1) | copy-start | bytes 28
  49.9 26.3 %copy-start.10 = (bf16[2,256,256]{2,1,0:T(8,128)(2,1)S(1)}, bf16[2,256,256]{2,1,0:T(8,128)(2,1)}, u32[]{:S(2)}) copy-start(bf16[2,256,256]{2,1,0:T(8,128)(2,1)} %constant.29.clone.table_z) | copy-start | bytes 786436
  49.9 26.3 %copy-start.16 = (f32[2,128,2048]{2,1,0:T(8,128)S(1)}, f32[2,128,2048]{2,1,0:T(8,128)}, u32[]{:S(2)}) copy-start(f32[2,128,2048]{2,1,0:T(8,128)} %copy-done.15) | copy-start | bytes 6291460
  114.0 11.1 %all-to-all-start.2 = ((f32[16,8,128]{2,1,0:T(8,128)}), f32[16,8,128]{2,1,0:T(8,128)S(1)}, u32[]{:S(2)}, u32[]{:S(2)}) async-start(f32[16,8,128]{2,1,0:T(8,128)} %bitcast.4), calls=%async_computation.2 | async-start | bytes 131072 | tf_op jit(solution)/shard_map/all_to_all | solution.py:505

commit v2 on v1

v2 whole, which is shorter than its diff:
```python
import jax
import jax.numpy as jnp
import ml_dtypes
import numpy as np
from jax import lax
from jax.experimental import pallas as pl
from jax.experimental.pallas import tpu as pltpu
from jax.sharding import PartitionSpec as P

f32 = jnp.float32
bf16 = jnp.bfloat16

STEPS = 2
CENTER = 5.0
HALF = 4.0
FRAGS = 2
TILES = 8
ENTRIES = FRAGS * TILES
N = 256
GROUPS = 8
OWNERS = 16
PEERS = GROUPS * OWNERS
PLANES = N // GROUPS
ROWS = N // OWNERS
CELLS = PLANES * ROWS
ORB = 128
BASIS = 1024
POINTS = TILES * N
MSG = 9
BOTH = ("frag", "grid")

NN = (((1,), (0,)), ((), ()))
NT = (((1,), (1,)), ((), ()))
TN = (((0,), (0,)), ((), ()))


def sine_table():
    index = np.arange(1, N + 1)
    phase = np.outer(index, index) % (2 * (N + 1))
    return np.sqrt(2.0 / (N + 1)) * np.sin(np.pi * phase / (N + 1))


def eigen_values():
    return 4.0 * np.sin(np.pi * np.arange(1, N + 1) / (2.0 * (N + 1))) ** 2


def halves(table):
    table = table.astype(np.float32)
    high = table.astype(ml_dtypes.bfloat16)
    low = (table - high.astype(np.float32)).astype(ml_dtypes.bfloat16)
    return jnp.asarray(np.stack([high, low]))


def dot(a, b, dims=NN):
    return lax.dot_general(a, b, dims, preferred_element_type=f32)


def split(x):
    high = x.astype(bf16)
    return high, (x - high.astype(f32)).astype(bf16)


def split3(x):
    high = x.astype(bf16)
    rest = x - high.astype(f32)
    middle = rest.astype(bf16)
    return high, middle, (rest - middle.astype(f32)).astype(bf16)


def dot3(a, b, dims=NN):
    return dot(a[0], b[0], dims) + (dot(a[0], b[1], dims) + dot(a[1], b[0], dims))


def spread(x):
    return jnp.broadcast_to(x, (8, 128))


def tree_sum(terms):
    terms = list(terms)
    while len(terms) > 1:
        terms = [
            terms[i] + terms[i + 1] if i + 1 < len(terms) else terms[i]
            for i in range(0, len(terms), 2)
        ]
    return terms[0]


def lane_columns(x, k):
    return [spread(x[:, k + j : k + j + 1]) for j in range(8)]


def inverse_factors(gram, factors, members):
    lane = lax.broadcasted_iota(jnp.int32, (8, 128), 1)
    sub = lax.broadcasted_iota(jnp.int32, (8, 128), 0)
    size = 32
    blocks = size // 8
    for first in range(0, ORB, size):
        end = first + size
        rows = [
            [gram[f, first + 8 * q : first + 8 * q + 8, :] for q in range(blocks)]
            for f in members
        ]
        done = [[None] * blocks for _ in members]
        pivots = [lane_columns(rows[f][0], first) for f in range(len(members))]
        for p in range(blocks):
            k = first + 8 * p
            last = p == blocks - 1
            inside = (lane >= k) & (lane < k + 8)
            unit = jnp.where(lane - k == sub, 1.0, 0.0)
            panel = [jnp.where(inside, unit, rows[f][p]) for f in range(len(members))]
            ahead = [[] if last else lane_columns(rows[f][p], k + 8) for f in range(len(members))]
            factor = [jnp.zeros((8, 128), f32)] * len(members)
            inverse = [[] for _ in members]
            for j in range(8):
                for f in range(len(members)):
                    column = pivots[f]
                    pivot = spread(column[j][j : j + 1, :])
                    inverse[f].append(1.0 / pivot)
                    row = spread(panel[f][j : j + 1, :])
                    factor[f] = jnp.where(sub == j, row * lax.rsqrt(pivot), factor[f])
                    ratio = jnp.where(sub == j, 0.0, column[j]) * inverse[f][j]
                    for i in range(j + 1, 8):
                        column[i] = column[i] - ratio * spread(column[i][j : j + 1, :])
                    for i in range(len(ahead[f])):
                        ahead[f][i] = ahead[f][i] - ratio * spread(ahead[f][i][j : j + 1, :])
                    panel[f] = panel[f] - ratio * row
            for f in range(len(members)):
                factors[members[f], k : k + 8, :] = jnp.where(lane < k + 8, factor[f], 0.0)
                done[f][p] = jnp.where((lane >= k + 8) & (lane < end), 0.0, factor[f])
                if last:
                    continue
                below = rows[f][p + 1]
                solved = [spread(panel[f][i : i + 1, :]) for i in range(8)]
                scaled = [c * r for c, r in zip(lane_columns(below, k), inverse[f])]
                pivots[f] = [
                    c - tree_sum([scaled[i] * spread(ahead[f][j][i : i + 1, :]) for i in range(8)])
                    for j, c in enumerate(lane_columns(below, k + 8))
                ]
                rows[f][p + 1] = jnp.where(inside, 0.0, below) - tree_sum(
                    [c * r for c, r in zip(scaled, solved)]
                )
                solved = [c * r for c, r in zip(solved, inverse[f])]
                for q in range(p + 2, blocks):
                    below = rows[f][q]
                    rows[f][q] = jnp.where(inside, 0.0, below) - tree_sum(
                        [c * r for c, r in zip(lane_columns(below, k), solved)]
                    )
            yield
        if end == ORB:
            continue
        lanes = lax.broadcasted_iota(jnp.int32, (ORB - end, 128), 1)
        passed = (lanes >= first) & (lanes < end)
        for f in range(len(members)):
            high, middle, low = split3(jnp.concatenate(done[f], axis=0))
            left = jnp.concatenate([high, high, middle, middle, high, low], axis=0)
            right = jnp.concatenate([high, middle, high, middle, low, high], axis=0)
            update = dot(left, right, TN)
            gram[members[f], end:, :] = jnp.where(passed, 0.0, gram[members[f], end:, :]) - update[end:, :]


def run(*works):
    works = list(works)
    while works:
        for work in tuple(works):
            if next(work, works) is works:
                works.remove(work)


def line_index(ids, counts, e):
    f, t = divmod(e, TILES)
    return jnp.where(t < counts[f], ids[f, t], -1)


def live_rows(counts, f):
    slot = lax.broadcasted_iota(jnp.int32, (TILES, N), 0)
    return (slot < counts[f]).astype(f32)


def density_lines(values, lines, f):
    row = 2.0 * jnp.sum(values * values, axis=0, keepdims=True)
    for t in range(TILES):
        lines[f * TILES + t : f * TILES + t + 1, :] = row[:, t * N : (t + 1) * N]


def start_kernel(
    ids, counts, start, ground, table_z, basis, send, orbitals,
    held, sem, gram, factors, lines,
):
    copies = [pltpu.make_async_copy(basis.at[f], held.at[f], sem.at[f]) for f in range(FRAGS)]
    for copy in copies:
        copy.start()
    eye = (
        lax.broadcasted_iota(jnp.int32, (ORB, ORB), 0)
        == lax.broadcasted_iota(jnp.int32, (ORB, ORB), 1)
    ).astype(f32).astype(bf16)
    turned = []
    for f in range(FRAGS):
        across = dot(eye, start[f], NT).astype(bf16)
        turned.append(across)
        gram[f] = dot(across, across, NT)

    def ground_modes():
        for z in range(2):
            rows = slice(z * PEERS, (z + 1) * PEERS)
            for g in range(4):
                values = split(ground[g * 128 : (g + 1) * 128, :])
                send[pl.ds(z * 4 + g, PEERS, stride=MSG), :] = dot3(
                    (table_z[0, rows, :], table_z[1, rows, :]), values, NT
                )
                yield

    run(inverse_factors(gram, factors, (0, 1)), ground_modes())
    charges = []
    for f in range(FRAGS):
        parts = split3(factors[f])
        rotated = dot(parts[0], turned[f]) + (dot(parts[1], turned[f]) + dot(parts[2], turned[f]))
        rounded = rotated.astype(bf16)
        orbitals[f] = rounded
        copies[f].wait()
        density_lines(dot(rounded, held[f], NT), lines, f)
        live = live_rows(counts, f)
        density = lines[f * TILES : (f + 1) * TILES, :] * live
        mean = jnp.sum(density) / (counts[f] * N).astype(f32)
        charges.append((density - mean) * live)
    charge = jnp.concatenate(charges, axis=0)
    blank = jnp.zeros((ENTRIES, N), f32)
    message = jnp.zeros((PEERS, 128), f32)
    for z in range(2):
        padded = jnp.concatenate([charge if i == z else blank for i in range(8)], axis=0)
        rows = slice(z * PEERS, (z + 1) * PEERS)
        message = message + dot3((table_z[0, rows, :], table_z[1, rows, :]), split(padded), NT)
    lane = lax.broadcasted_iota(jnp.int32, (1, 128), 1)
    label = jnp.zeros((1, 128), f32)
    for e in range(ENTRIES):
        label = jnp.where(lane == 2 * ENTRIES + e, line_index(ids, counts, e).astype(f32), label)
    send[pl.ds(8, PEERS, stride=MSG), :] = message + label


def exchange_chunks(parts):
    place = lax.broadcasted_iota(jnp.int32, (8, 128), 1) >> 4
    moved = [parts[0]] + [pltpu.roll(parts[i], 16 * i, 1) for i in range(1, 8)]
    results = []
    for j in range(8):
        total = moved[0]
        for i in range(1, 8):
            total = jnp.where(place == (i + j) % 8, moved[i], total)
        results.append(total if j == 0 else pltpu.roll(total, 128 - 16 * j, 1))
    return results


def turn_kernel(first, basis, kinetic, turned, collocated, applied):
    vector = first[0]
    across = basis[0].T
    turned[0] = across
    collocated[0] = dot(vector, across)
    applied[0] = dot(vector, kinetic[0])


def line_masks():
    row = lax.broadcasted_iota(jnp.int32, (128, 128), 0)
    lane = lax.broadcasted_iota(jnp.int32, (128, 128), 1)
    repeats = [
        (row == part * ENTRIES + (lane & 15)).astype(f32).astype(bf16) for part in range(3)
    ]
    own = (lane >> 4) == (row & 7)
    group = lax.broadcasted_iota(jnp.int32, (16, 128), 0)
    member = lax.broadcasted_iota(jnp.int32, (16, 128), 1) >> 3
    return repeats, own, (group == member).astype(f32).astype(bf16)


def solve_kernel(
    arrived, table, table_p, table_pt, eigen, eigen_z, send, plane, wanted,
):
    repeats, own, members = line_masks()
    labels = arrived[pl.ds(8, PEERS, stride=MSG), :]
    index = labels.astype(jnp.int32)
    plane_x = jnp.where(index < 0, 2 * PLANES, (index >> 8) & (PLANES - 1))
    cell_y = index & (N - 1)
    high, low = split(labels)
    both = jnp.concatenate(repeats[:2], axis=1)
    spread_high, spread_low = dot(high, both), dot(low, both)
    pieces = [
        spread_high[:, :128],
        spread_low[:, :128],
        spread_high[:, 128:],
        spread_low[:, 128:],
        dot(plane_x.astype(f32).astype(bf16), repeats[2]),
        dot(cell_y.astype(f32).astype(bf16), repeats[2]),
    ]
    masked = jnp.concatenate([jnp.where(own, piece, 0.0) for piece in pieces], axis=1)
    grouped = dot(members, masked.astype(bf16))

    def line_row(fq, part):
        lanes = slice(part * 128, (part + 1) * 128)
        return jnp.concatenate(
            [grouped[2 * fq + half : 2 * fq + half + 1, lanes] for half in range(2)], axis=1
        )

    sub_x = lax.broadcasted_iota(jnp.int32, (PLANES, N), 0).astype(f32)
    sub_y = lax.broadcasted_iota(jnp.int32, (N, N), 0).astype(f32)
    here = []
    for fq in range(GROUPS):
        wanted[fq] = (line_row(fq, 5) == sub_y).astype(f32).astype(bf16)
        here.append(line_row(fq, 4) == sub_x)
        values = jnp.concatenate(
            [jnp.where(here[fq], line_row(fq, part), 0.0) for part in range(4)], axis=0
        )
        placed = dot(values.astype(bf16), wanted[fq], NT)
        for z in range(2):
            base = z * 2 * PLANES
            total = placed[base : base + PLANES] + placed[base + PLANES : base + 2 * PLANES]
            for half in range(2):
                plane[pl.ds((z * 2 + half) * N + fq, PLANES, stride=GROUPS), :] = total[
                    :, half * 128 : (half + 1) * 128
                ]
    chunks = [(z, half, g) for z in range(2) for half in range(2) for g in range(4)]
    for z, half, g in chunks:
        parts = exchange_chunks(
            [
                arrived[pl.ds((half * 8 + i) * MSG + z * 4 + g, 8, stride=OWNERS * MSG), :]
                for i in range(8)
            ]
        )
        for i in range(8):
            row = (z * 2 + half) * N + (g * 8 + i) * 8
            plane[row : row + 8, :] = plane[row : row + 8, :] - parts[i]
    table_y = (table[0], table[1])
    forward = (table_p[0], table_p[1])
    backward = (table_pt[0], table_pt[1])
    source = jnp.concatenate(
        [
            jnp.concatenate([plane[z * 2 * N + half * N :][:N] for half in range(2)], axis=1)
            for z in range(2)
        ],
        axis=0,
    )
    along_y = dot3(split(source), table_y)
    modes = []
    for z in range(2):
        mode = dot3(forward, split(along_y[z * N : (z + 1) * N])) / (eigen[...] + eigen_z[z])
        modes.append(dot3(backward, split(mode)))
    values = dot3(split(jnp.concatenate(modes, axis=0)), table_y)
    for z in range(2):
        for half in range(2):
            plane[(z * 2 + half) * N : (z * 2 + half + 1) * N, :] = values[
                z * N : (z + 1) * N, half * 128 : (half + 1) * 128
            ]
    for z, half, g in chunks:
        base = (z * 2 + half) * N + g * 64
        parts = exchange_chunks([plane[base + 8 * i : base + 8 * i + 8, :] for i in range(8)])
        for i in range(8):
            send[pl.ds((half * 8 + i) * MSG + z * 4 + g, 8, stride=OWNERS * MSG), :] = parts[i]
    found = [[], []]
    for fq in range(GROUPS):
        stack = []
        for z in range(2):
            rows = jnp.concatenate(
                [
                    plane[pl.ds((z * 2 + half) * N + fq, PLANES, stride=GROUPS), :]
                    for half in range(2)
                ],
                axis=1,
            )
            stack.extend(split(rows))
        columns = dot(jnp.concatenate(stack, axis=0), wanted[fq])
        for z in range(2):
            base = z * 2 * PLANES
            total = columns[base : base + PLANES] + columns[base + PLANES : base + 2 * PLANES]
            line = jnp.sum(jnp.where(here[fq], total, 0.0), axis=0, keepdims=True)
            found[z].extend([line[:, :128], line[:, 128:]])
    reply = jnp.zeros((PEERS, 128), f32)
    for z in range(2):
        for piece in split(jnp.concatenate(found[z], axis=0)):
            spread_lines = jnp.where(own, dot(members, piece, TN), 0.0)
            reply = reply + dot(spread_lines.astype(bf16), repeats[z], NT)
    send[pl.ds(8, PEERS, stride=MSG), :] = reply


def cycle_kernel(
    ids, counts, degrees, arrived, table_z, first, first_collocated, first_applied,
    basis, turned, kinetic, send,
    held, held_turned, held_kinetic, sem, field, orbitals, weighted, following, gram, factors,
    lines,
):
    copies = []
    for f in range(FRAGS):
        copies.append(
            [
                pltpu.make_async_copy(source.at[f], target.at[f], sem.at[3 * f + i])
                for i, (source, target) in enumerate(
                    ((basis, held), (turned, held_turned), (kinetic, held_kinetic))
                )
            ]
        )
    for three in copies:
        for copy in three:
            copy.start()
    spectrum = arrived[pl.ds(8, PEERS, stride=MSG), :].T
    values = jnp.zeros((ENTRIES, N), f32)
    for z in range(2):
        rows = slice(z * PEERS, (z + 1) * PEERS)
        values = values + dot3(
            split(spectrum[z * ENTRIES : (z + 1) * ENTRIES, :]),
            (table_z[0, rows, :], table_z[1, rows, :]),
        )
    for f in range(FRAGS):
        field[f * TILES : (f + 1) * TILES, :] = (
            values[f * TILES : (f + 1) * TILES] * live_rows(counts, f)
        )

    wide = 2 * N
    parts = BASIS // N

    def weigh(f, part, points):
        tile = f * TILES + 2 * part
        weights = jnp.concatenate([field[tile + t : tile + t + 1, :] for t in range(2)], axis=1)
        weighted[f, :, part * wide : (part + 1) * wide] = (points * weights).astype(bf16)

    def to_grid(f, vector):
        for part in range(POINTS // wide):
            weigh(f, part, dot(vector, held_turned[f, :, part * wide : (part + 1) * wide]))
            yield

    def filtered(f, step):
        if step == 0:
            orbitals[f] = first[f]
            copies[f][0].wait()
            for part in range(POINTS // wide):
                weigh(f, part, first_collocated[f, :, part * wide : (part + 1) * wide])
                yield
        else:
            yield from to_grid(f, orbitals[f])
        tiles = [slice(part * N, (part + 1) * N) for part in range(parts)]
        for tile in tiles:
            earlier = orbitals[f, :, tile].astype(f32)
            if step == 0:
                local = first_applied[f, :, tile]
            else:
                local = dot(orbitals[f], held_kinetic[f, :, tile])
            product = local + dot(weighted[f], held[f, :, tile])
            following[f, :, tile] = (product - CENTER * earlier) / HALF
            yield
        vector = following[f].astype(bf16)
        if step == 0:
            copies[f][1].wait()
            copies[f][2].wait()
        yield from to_grid(f, vector)
        total = jnp.zeros((ORB, ORB), f32)
        for tile in tiles:
            earlier = orbitals[f, :, tile].astype(f32)
            product = dot(vector, held_kinetic[f, :, tile]) + dot(weighted[f], held[f, :, tile])
            second = (
                2.0 * (product - CENTER * vector[:, tile].astype(f32)) / HALF - earlier
            )
            chosen = jnp.where(degrees[f] == 2, second, following[f, :, tile])
            following[f, :, tile] = chosen
            yield
            total = total + lax.dot_general(
                chosen, chosen, NT, precision=lax.Precision.HIGHEST, preferred_element_type=f32
            )
            yield
        gram[f] = total

    def rotated(f):
        for part in range(parts):
            tile = slice(part * N, (part + 1) * N)
            orbitals[f, :, tile] = lax.dot_general(
                factors[f], following[f, :, tile], NN,
                precision=lax.Precision.HIGHEST, preferred_element_type=f32,
            ).astype(bf16)
            yield

    def new_density(f):
        for part in range(POINTS // wide):
            values = dot(orbitals[f], held_turned[f, :, part * wide : (part + 1) * wide])
            row = 2.0 * jnp.sum(values * values, axis=0, keepdims=True)
            for t in range(2):
                line = f * TILES + 2 * part + t
                lines[line : line + 1, :] = row[:, t * N : (t + 1) * N]
            yield

    def chain(*works):
        for work in works:
            yield from work

    run(filtered(0, 0))
    for step in range(STEPS):
        run(inverse_factors(gram, factors, (0,)), filtered(1, step))
        if step < STEPS - 1:
            follow = chain(rotated(0), filtered(0, step + 1))
        else:
            follow = chain(rotated(0), new_density(0))
        run(inverse_factors(gram, factors, (1,)), follow)
        run(rotated(1))
    run(new_density(1))
    send[...] = jnp.full((OWNERS * 8, 128), -1.0, f32)
    line_of = [line_index(ids, counts, e) for e in range(ENTRIES)]
    owner_of = [jnp.where(line >= 0, (line & (N - 1)) >> 4, -1) for line in line_of]
    for e in range(ENTRIES):
        rank = jnp.int32(0)
        for i in range(e):
            rank = rank + jnp.where(owner_of[i] == owner_of[e], 1, 0)
        rank = jnp.minimum(rank, 1)
        local = ((line_of[e] >> 8) & (PLANES - 1)) * ROWS + (line_of[e] & (ROWS - 1))

        @pl.when(line_of[e] >= 0)
        def _():
            base = owner_of[e] * 8
            for half in range(2):
                send[pl.ds(base + rank * 2 + half, 1), :] = lines[
                    e : e + 1, half * 128 : (half + 1) * 128
                ]
            send[pl.ds(base + 4 + rank, 1), :] = jnp.full((1, 128), local.astype(f32))


def potential_kernel(arrived, table_z, potential, modes):
    for z in range(2):
        for g in range(4):
            modes[z * PEERS : (z + 1) * PEERS, g * 128 : (g + 1) * 128] = arrived[
                pl.ds(z * 4 + g, PEERS, stride=MSG), :
            ]
    potential[...] = dot3(split(modes[...]), (table_z[0], table_z[1]), TN)


def density_kernel(arrived, density):
    lane = lax.broadcasted_iota(jnp.int32, (OWNERS, CELLS), 1)
    masks, values = [], []
    for slot in range(2):
        index = arrived[pl.ds(4 + slot, OWNERS, stride=8), :].astype(jnp.int32)
        masks.append(
            (jnp.concatenate([index] * (CELLS // 128), axis=1) == lane).astype(f32)
        )
        values.append(
            jnp.concatenate(
                [arrived[pl.ds(slot * 2 + half, OWNERS, stride=8), :] for half in range(2)],
                axis=1,
            )
        )
    mask = jnp.concatenate(masks, axis=0).astype(bf16)
    parts = split3(jnp.concatenate(values, axis=0))
    density[...] = dot(mask, parts[0], TN) + (dot(mask, parts[1], TN) + dot(mask, parts[2], TN))


VM = pl.BlockSpec(memory_space=pltpu.VMEM)
SM = pl.BlockSpec(memory_space=pltpu.SMEM)
ANY = pl.BlockSpec(memory_space=pl.ANY)


def call(kernel, name, in_specs, shapes, scratch, operands, flops=0, limit=40):
    outs = [jax.ShapeDtypeStruct(shape, dtype) for shape, dtype in shapes]
    single = len(outs) == 1
    return pl.pallas_call(
        kernel,
        out_shape=outs[0] if single else outs,
        in_specs=in_specs,
        out_specs=VM if single else [VM] * len(outs),
        scratch_shapes=scratch,
        name=name,
        cost_estimate=pl.CostEstimate(flops=flops, bytes_accessed=1 << 20, transcendentals=0),
        compiler_params=pltpu.CompilerParams(vmem_limit_bytes=limit << 20),
    )(*operands)


def trade(message):
    packed = message.reshape(PEERS, MSG, 1, 128)
    return lax.all_to_all(packed, BOTH, 0, 0, tiled=True).reshape(PEERS * MSG, 128)


def shards(kinetic, basis, start_orbitals, background, tile_ids, tile_counts, degrees):
    sines = sine_table()
    eigen = eigen_values()
    order_z = np.concatenate([np.arange(0, N, 2), np.arange(1, N, 2)])
    row = np.arange(N)
    order_x = (row % GROUPS) * PLANES + row // GROUPS
    table_z = halves(sines[order_z])
    table_y = halves(sines)
    table_p = halves(sines[:, order_x])
    table_pt = halves(sines[order_x, :])
    eigen_xy = jnp.asarray((eigen[:, None] + eigen[None, :]).astype(np.float32))
    device = lax.axis_index("frag") * OWNERS + lax.axis_index("grid")
    eigen_z = lax.dynamic_slice(jnp.asarray(eigen.astype(np.float32)), (2 * device,), (2,))

    dma = pltpu.SemaphoreType.DMA
    square = pltpu.VMEM((FRAGS, ORB, ORB), f32)
    message_a, first = call(
        start_kernel, "start",
        [SM, SM, VM, VM, VM, ANY],
        [((PEERS * MSG, 128), f32), ((FRAGS, ORB, BASIS), bf16)],
        [
            pltpu.VMEM((FRAGS, POINTS, BASIS), bf16),
            dma((FRAGS,)),
            square,
            square,
            pltpu.VMEM((ENTRIES, N), f32),
        ],
        (tile_ids, tile_counts, start_orbitals, background.reshape(CELLS, N), table_z, basis),
        flops=10**10, limit=60,
    )
    arrived_a = trade(message_a)
    part = POINTS // 4
    turned, collocated, applied = pl.pallas_call(
        turn_kernel,
        grid=(FRAGS, 4),
        out_shape=[
            jax.ShapeDtypeStruct((FRAGS, BASIS, POINTS), bf16),
            jax.ShapeDtypeStruct((FRAGS, ORB, POINTS), f32),
            jax.ShapeDtypeStruct((FRAGS, ORB, BASIS), f32),
        ],
        in_specs=[
            pl.BlockSpec((1, ORB, BASIS), lambda f, i: (f, 0, 0)),
            pl.BlockSpec((1, part, BASIS), lambda f, i: (f, i, 0)),
            pl.BlockSpec((1, BASIS, BASIS // 4), lambda f, i: (f, 0, i)),
        ],
        out_specs=[
            pl.BlockSpec((1, BASIS, part), lambda f, i: (f, 0, i)),
            pl.BlockSpec((1, ORB, part), lambda f, i: (f, 0, i)),
            pl.BlockSpec((1, ORB, BASIS // 4), lambda f, i: (f, 0, i)),
        ],
        name="turn",
        cost_estimate=pl.CostEstimate(flops=10**10, bytes_accessed=24 << 20, transcendentals=0),
        compiler_params=pltpu.CompilerParams(vmem_limit_bytes=60 << 20),
    )(first, basis, kinetic)
    arrived_a, turned, collocated, applied = lax.optimization_barrier(
        (arrived_a, turned, collocated, applied)
    )
    message_b = call(
        solve_kernel, "solve",
        [VM, VM, VM, VM, VM, SM],
        [((PEERS * MSG, 128), f32)],
        [pltpu.VMEM((4 * N, 128), f32), pltpu.VMEM((GROUPS, N, N), bf16)],
        (arrived_a, table_y, table_p, table_pt, eigen_xy, eigen_z),
        flops=5 * 10**9, limit=24,
    )
    arrived_b = trade(message_b)
    message_c = call(
        cycle_kernel, "cycle",
        [SM, SM, SM, VM, VM, VM, VM, VM, ANY, ANY, ANY],
        [((OWNERS * 8, 128), f32)],
        [
            pltpu.VMEM((FRAGS, POINTS, BASIS), bf16),
            pltpu.VMEM((FRAGS, BASIS, POINTS), bf16),
            pltpu.VMEM((FRAGS, BASIS, BASIS), bf16),
            dma((3 * FRAGS,)),
            pltpu.VMEM((ENTRIES, N), f32),
            pltpu.VMEM((FRAGS, ORB, BASIS), bf16),
            pltpu.VMEM((FRAGS, ORB, POINTS), bf16),
            pltpu.VMEM((FRAGS, ORB, BASIS), f32),
            square,
            square,
            pltpu.VMEM((ENTRIES, N), f32),
        ],
        (
            tile_ids, tile_counts, degrees, arrived_b, table_z, first, collocated, applied,
            basis, turned, kinetic,
        ),
        flops=4 * 10**10, limit=40,
    )
    arrived_c = lax.all_to_all(
        message_c.reshape(OWNERS, 8, 128), "grid", 0, 0, tiled=True
    ).reshape(OWNERS * 8, 128)
    potential = call(
        potential_kernel, "potential", [VM, VM], [((CELLS, N), f32)],
        [pltpu.VMEM((2 * PEERS, CELLS), f32)], (arrived_b, table_z), flops=10**9,
    )
    density = call(
        density_kernel, "density", [VM], [((CELLS, N), f32)], [], (arrived_c,), flops=10**8,
    )
    return potential.reshape(PLANES, ROWS, N), density.reshape(PLANES, ROWS, N)


def solution(mesh):
    in_specs = (
        P(BOTH, None, None),
        P(BOTH, None, None),
        P(BOTH, None, None),
        P("frag", "grid", None),
        P(BOTH, None),
        P(BOTH),
        P(BOTH),
    )
    out_specs = (P("frag", "grid", None), P("frag", "grid", None))
    return jax.shard_map(shards, mesh=mesh, in_specs=in_specs, out_specs=out_specs, check_vma=False)
```

time: 127 us -> 103 us (0.81)
  waiting for transfers between devices: 20.3 us -> 8.55 us
  local copies, waits for them, and re-layouts: 9.2 us -> 0.14 us
  Pallas kernels: 62.7 us -> 57 us
  blocking collectives: 18.5 us -> 21.7 us
    pallas_call x5, Pallas kernels: 62.7 us -> 45 us  [call(): pl.pallas_call(kernel, out_shape=outs[0] if single else outs, in_specs=in...]
    pallas_call x0 -> x1, Pallas kernels: none -> 12 us  [shards(): pl.pallas_call(turn_kernel, grid=(FRAGS, 4), out_shape=[jax.ShapeDtypeStr...]
    all_to_all x1, waiting for transfers between devices: 14 us -> 2.16 us  [trade(): lax.all_to_all(packed, BOTH, 0, 0, tiled=True).reshape(PEERS * MSG, 128)]
    unnamed x36 -> x26, local copies, waits for them, and re-layouts: 9.12 us -> 0.07 us
    all_to_all x1, blocking collectives: 18.5 us -> 21.7 us  [trade(): lax.all_to_all(packed, BOTH, 0, 0, tiled=True).reshape(PEERS * MSG, 128)]
  transfers between devices with their start and end apart: 2 -> 2, of which waited for: 2 -> 2; matrix products, arithmetic and copies ran while one was open for 0% -> 0% of each run, Pallas kernels for 1% -> 13%
where the time goes in v2:
time: 103 us
  Pallas kernels  57 us (55%)
  blocking collectives  21.7 us (21%)
  starting transfers between devices  14.7 us (14%)
  waiting for transfers between devices  8.55 us (8%)
    pallas_call x5, Pallas kernels, call(): pl.pallas_call(kernel, out_shape=outs[0] if single else outs, in_specs=in...  45 us
    all_to_all x1, blocking collectives, trade(): lax.all_to_all(packed, BOTH, 0, 0, tiled=True).reshape(PEERS * MSG, 128)  21.7 us
    pallas_call x1, Pallas kernels, shards(): pl.pallas_call(turn_kernel, grid=(FRAGS, 4), out_shape=[jax.ShapeDtypeStr...  12 us
    all_to_all x1, starting transfers between devices, trade(): lax.all_to_all(packed, BOTH, 0, 0, tiled=True).reshape(PEERS * MSG, 128)  11.2 us
    all_to_all x1, waiting for transfers between devices, shards(): lax.all_to_all(message_c.reshape(OWNERS, 8, 128), 'grid', 0, 0, tiled=True)  6.39 us
    all_to_all x1, starting transfers between devices, shards(): lax.all_to_all(message_c.reshape(OWNERS, 8, 128), 'grid', 0, 0, tiled=True)  3.51 us
    all_to_all x1, waiting for transfers between devices, trade(): lax.all_to_all(packed, BOTH, 0, 0, tiled=True).reshape(PEERS * MSG, 128)  2.16 us
  transfers between devices with their start and end apart: 2, of which 2 were waited for; matrix products, arithmetic and copies ran while one was open for 0% of the time, Pallas kernels for 13%

profile of v2, /device:TPU:0, one launch (start us, length us, event | category | flops | bytes accessed | tf_op | source)
XLA Modules:
  0.0 102.9 jit_solution(13841331754503150749)
XLA Ops:
  0.6 0.0 copy-start.12
  0.6 12.2 %start.2 = (f32[1152,128]{1,0:T(8,128)}, bf16[2,128,1024]{2,1,0:T(8,128)(2,1)}) custom-call(s32[2,8]{1,0:T(2,128)} %ids.3, s32[2]{0:T(128)} %counts.3, bf16[2,1024,128]{2,1,0:T(8,128)(2,1)} %start.3, f32[512,256]{1,0:T(8,128)} %bitcast.16, bf16[2,256,256]{2,1,0:T(8,128)(2,1)} %constant.29.clone.table_z, bf16[2,2048,1024]{2,1,0:T(8,128)(2,1)} %basis.5), custom_call_target="tpu_custom_call" | custom-call | flops 10000000000 | bytes 1048576 | tf_op jit(solution)/shard_map/start/pallas_call | solution.py:552
  12.8 11.2 %all-to-all-start = ((f32[128,9,1,128]{3,2,1,0:T(1,128)}), f32[128,9,1,128]{3,2,1,0:T(1,128)S(1)}, u32[]{:S(2)}, u32[]{:S(2)}) async-start(f32[128,9,1,128]{3,2,1,0:T(1,128)} %bitcast.14), calls=%async_computation | async-start | bytes 1179648 | tf_op jit(solution)/shard_map/all_to_all | solution.py:566
  24.0 0.0 copy-done.12
  24.0 0.1 dynamic_slice.3.eigen_z
  24.1 12.0 %turn.1 = (bf16[2,1024,2048]{2,1,0:T(8,128)(2,1)}, f32[2,128,2048]{2,1,0:T(8,128)}, f32[2,128,1024]{2,1,0:T(8,128)}) custom-call(bf16[2,128,1024]{2,1,0:T(8,128)(2,1)} %get-tuple-element.12.first, bf16[2,2048,1024]{2,1,0:T(8,128)(2,1)} %basis.5, bf16[2,1024,1024]{2,1,0:T(8,128)(2,1)} %kinetic.3), custom_call_target="tpu_custom_call" | custom-call | flops 10000000000 | bytes 25165824 | tf_op jit(solution)/shard_map/turn/pallas_call | solution.py:601
  36.1 2.2 %all-to-all-done = f32[128,9,1,128]{3,2,1,0:T(1,128)S(1)} async-done(((f32[128,9,1,128]{3,2,1,0:T(1,128)}), f32[128,9,1,128]{3,2,1,0:T(1,128)S(1)}, u32[]{:S(2)}, u32[]{:S(2)}) %all-to-all-start) | async-done | bytes 589856 | tf_op jit(solution)/shard_map/all_to_all | solution.py:566
  38.3 0.0 copy-done.5
  38.3 0.0 copy-done.6
  38.3 0.0 copy-done.7
  38.3 0.0 copy-start
  38.3 0.0 copy-start.1
  38.3 0.0 copy-start.2
  38.3 0.0 copy-start.3
  38.3 0.0 copy-start.4
  38.4 0.0 copy-start.11
  38.4 4.3 %solve.1 = f32[1152,128]{1,0:T(8,128)S(1)} custom-call(f32[1152,128]{1,0:T(8,128)S(1)} %bitcast.9, bf16[2,256,256]{2,1,0:T(8,128)(2,1)S(1)} %copy-done.8, bf16[2,256,256]{2,1,0:T(8,128)(2,1)S(1)} %copy-done.7, bf16[2,256,256]{2,1,0:T(8,128)(2,1)S(1)} %copy-done.6, f32[256,256]{1,0:T(8,128)S(1)} %copy-done.5, f32[2]{0:T(128)S(1)} %dynamic_slice.3.eigen_z), custom_call_target="tpu_custom_call" | custom-call | flops 5000000000 | bytes 1048576 | tf_op jit(solution)/shard_map/solve/pallas_call | solution.py:552
  42.7 21.7 %all_to_all.15 = f32[128,9,1,128]{3,2,1,0:T(1,128)S(1)} all-to-all(f32[128,9,1,128]{3,2,1,0:T(1,128)S(1)} %bitcast.12), channel_id=1, replica_groups=mesh['frag'=8,'grid'=16] {'frag','grid'}, dimensions={0} | all-to-all | bytes 1179648 | tf_op jit(solution)/shard_map/all_to_all | solution.py:566
  64.4 0.0 copy-done.1
  64.5 26.1 %cycle.1 = f32[128,128]{1,0:T(8,128)} custom-call(s32[2,8]{1,0:T(2,128)S(1)} %copy-done.1, s32[2]{0:T(128)S(1)} %copy-done.2, s32[2]{0:T(128)S(1)} %copy-done.3, f32[1152,128]{1,0:T(8,128)S(1)} %bitcast.10, bf16[2,256,256]{2,1,0:T(8,128)(2,1)S(1)} %copy-done.4, bf16[2,128,1024]{2,1,0:T(8,128)(2,1)S(1)} %copy-done.11, f32[2,128,2048]{2,1,0:T(8,128)S(1)} %copy-done.9, ...), custom_call_target="tpu_custom_call" | custom-call | flops 40000000000 | bytes 1048576 | tf_op jit(solution)/shard_map/cycle/pallas_call | solution.py:552
  90.5 3.5 %all-to-all-start.2 = ((f32[16,8,128]{2,1,0:T(8,128)}), f32[16,8,128]{2,1,0:T(8,128)S(1)}, u32[]{:S(2)}, u32[]{:S(2)}) async-start(f32[16,8,128]{2,1,0:T(8,128)} %bitcast.6), calls=%async_computation.2 | async-start | bytes 131072 | tf_op jit(solution)/shard_map/all_to_all | solution.py:658
  94.1 1.2 %potential.1 = f32[512,256]{1,0:T(8,128)} custom-call(f32[1152,128]{1,0:T(8,128)S(1)} %bitcast.11, bf16[2,256,256]{2,1,0:T(8,128)(2,1)S(1)} %copy-done.4), custom_call_target="tpu_custom_call" | custom-call | flops 1000000000 | bytes 1048576 | tf_op jit(solution)/shard_map/potential/pallas_call | solution.py:552
  95.3 6.4 %all-to-all-done.2 = f32[16,8,128]{2,1,0:T(8,128)S(1)} async-done(((f32[16,8,128]{2,1,0:T(8,128)}), f32[16,8,128]{2,1,0:T(8,128)S(1)}, u32[]{:S(2)}, u32[]{:S(2)}) %all-to-all-start.2) | async-done | bytes 65568 | tf_op jit(solution)/shard_map/all_to_all | solution.py:658
  101.7 1.2 %density.1 = f32[512,256]{1,0:T(8,128)} custom-call(f32[128,128]{1,0:T(8,128)S(1)} %bitcast.13), custom_call_target="tpu_custom_call" | custom-call | flops 100000000 | bytes 1048576 | tf_op jit(solution)/shard_map/density/pallas_call | solution.py:552
  (14 shorter events, 0.0 us)
Async XLA Ops:
  0.6 23.4 %copy-start.12 = (f32[256]{0:T(256)S(1)}, f32[256]{0:T(256)}, u32[]{:S(2)}) copy-start(f32[256]{0:T(256)} %constant.34.clone) | copy-start | bytes 3076
  12.8 25.4 %all-to-all-start = ((f32[128,9,1,128]{3,2,1,0:T(1,128)}), f32[128,9,1,128]{3,2,1,0:T(1,128)S(1)}, u32[]{:S(2)}, u32[]{:S(2)}) async-start(f32[128,9,1,128]{3,2,1,0:T(1,128)} %bitcast.14), calls=%async_computation | async-start | bytes 1179648 | tf_op jit(solution)/shard_map/all_to_all | solution.py:566
  24.1 14.2 %copy-start.5 = (f32[256,256]{1,0:T(8,128)S(1)}, f32[256,256]{1,0:T(8,128)}, u32[]{:S(2)}) copy-start(f32[256,256]{1,0:T(8,128)} %constant.33.clone.eigen) | copy-start | bytes 786436
  24.1 14.2 %copy-start.6 = (bf16[2,256,256]{2,1,0:T(8,128)(2,1)S(1)}, bf16[2,256,256]{2,1,0:T(8,128)(2,1)}, u32[]{:S(2)}) copy-start(bf16[2,256,256]{2,1,0:T(8,128)(2,1)} %constant.32.clone.table_pt) | copy-start | bytes 786436
  24.1 14.2 %copy-start.7 = (bf16[2,256,256]{2,1,0:T(8,128)(2,1)S(1)}, bf16[2,256,256]{2,1,0:T(8,128)(2,1)}, u32[]{:S(2)}) copy-start(bf16[2,256,256]{2,1,0:T(8,128)(2,1)} %constant.31.clone.table_p) | copy-start | bytes 786436
  24.1 14.2 %copy-start.8 = (bf16[2,256,256]{2,1,0:T(8,128)(2,1)S(1)}, bf16[2,256,256]{2,1,0:T(8,128)(2,1)}, u32[]{:S(2)}) copy-start(bf16[2,256,256]{2,1,0:T(8,128)(2,1)} %constant.30.clone.table) | copy-start | bytes 786436
  38.3 26.1 %copy-start = (bf16[2,1024,1024]{2,1,0:T(8,128)(2,1)S(1)}, bf16[2,1024,1024]{2,1,0:T(8,128)(2,1)}, u32[]{:S(2)}) copy-start(bf16[2,1024,1024]{2,1,0:T(8,128)(2,1)} %kinetic.3) | copy-start | bytes 12582916
  38.3 26.1 %copy-start.1 = (s32[2,8]{1,0:T(2,128)S(1)}, s32[2,8]{1,0:T(2,128)}, u32[]{:S(2)}) copy-start(s32[2,8]{1,0:T(2,128)} %ids.3) | copy-start | bytes 196
  38.3 26.1 %copy-start.2 = (s32[2]{0:T(128)S(1)}, s32[2]{0:T(128)}, u32[]{:S(2)}) copy-start(s32[2]{0:T(128)} %counts.3) | copy-start | bytes 28
  38.3 26.1 %copy-start.3 = (s32[2]{0:T(128)S(1)}, s32[2]{0:T(128)}, u32[]{:S(2)}) copy-start(s32[2]{0:T(128)} %degrees.1) | copy-start | bytes 28
  38.3 26.1 %copy-start.4 = (bf16[2,256,256]{2,1,0:T(8,128)(2,1)S(1)}, bf16[2,256,256]{2,1,0:T(8,128)(2,1)}, u32[]{:S(2)}) copy-start(bf16[2,256,256]{2,1,0:T(8,128)(2,1)} %constant.29.clone.table_z) | copy-start | bytes 786436
  38.3 26.1 %copy-start.9 = (f32[2,128,2048]{2,1,0:T(8,128)S(1)}, f32[2,128,2048]{2,1,0:T(8,128)}, u32[]{:S(2)}) copy-start(f32[2,128,2048]{2,1,0:T(8,128)} %get-tuple-element.17.first_collocated) | copy-start | bytes 6291460
  38.4 26.1 %copy-start.10 = (f32[2,128,1024]{2,1,0:T(8,128)S(1)}, f32[2,128,1024]{2,1,0:T(8,128)}, u32[]{:S(2)}) copy-start(f32[2,128,1024]{2,1,0:T(8,128)} %get-tuple-element.18.first_applied) | copy-start | bytes 3145732
  38.4 26.1 %copy-start.11 = (bf16[2,128,1024]{2,1,0:T(8,128)(2,1)S(1)}, bf16[2,128,1024]{2,1,0:T(8,128)(2,1)}, u32[]{:S(2)}) copy-start(bf16[2,128,1024]{2,1,0:T(8,128)(2,1)} %get-tuple-element.12.first) | copy-start | bytes 1572868
  90.5 11.1 %all-to-all-start.2 = ((f32[16,8,128]{2,1,0:T(8,128)}), f32[16,8,128]{2,1,0:T(8,128)S(1)}, u32[]{:S(2)}, u32[]{:S(2)}) async-start(f32[16,8,128]{2,1,0:T(8,128)} %bitcast.6), calls=%async_computation.2 | async-start | bytes 131072 | tf_op jit(solution)/shard_map/all_to_all | solution.py:658
